TPU v7x, 256 devices: a whole 4x4x8 slice. The times are simulated.
256 devices in a mesh: ctx: 16 (over y, x_lo, core), head: 16 (over z, x_hi).
Axes of the slice: x: 4 (x_hi: 2, x_lo: 2; x = x_hi * 2 + x_lo), y: 4, z: 8, core: 2. Of those that a mesh axis runs over, the one named last changes fastest.
Arguments:
- query: bfloat16 [4096, 4096], P('ctx', 'head'), may hold values from -120 to 120
- keys: bfloat16 [4096, 4096], P('ctx', 'head'), may hold values from -9 to 9
- values: bfloat16 [4096, 4096], P('ctx', 'head'), may hold values from -6 to 6
- out_grad: bfloat16 [4096, 4096], P('ctx', 'head'), may hold values from -0.625 to 0.625
- gate_left: bfloat16 [4096, 512], P('head'), may hold values from -0.375 to 0.375
- up_left: bfloat16 [4096, 512], P('head'), may hold values from -0.375 to 0.375
- gate_right: bfloat16 [512, 11008], P(None, 'head'), may hold values from -0.25 to 0.25
- up_right: bfloat16 [512, 11008], P(None, 'head'), may hold values from -0.25 to 0.25
- down_left: bfloat16 [11008, 512], P('head'), may hold values from -0.25 to 0.25
- down_right: bfloat16 [512, 4096], P(None, 'head'), may hold values from -0.09375 to 0.09375
- block_order: int32 [32], replicated, may hold values from 0 to 31, each once
- doc_lengths: int32 [4], replicated, may hold values from 1 to 2048, 4096 in all
Outputs:
- grad_query: bfloat16 [4096, 4096], P('ctx', 'head')
- grad_keys: bfloat16 [4096, 4096], P('ctx', 'head')
- grad_values: bfloat16 [4096, 4096], P('ctx', 'head')
- grad_gate_left: float32 [4096, 512], P('head', 'ctx')
- grad_up_left: float32 [4096, 512], P('head', 'ctx')
- grad_down_left: float32 [11008, 512], P('head', 'ctx')
- grad_gate_right: float32 [512, 11008], P('ctx', 'head')
- grad_up_right: float32 [512, 11008], P('ctx', 'head')
- grad_down_right: float32 [512, 4096], P('ctx', 'head')
All inputs are finite; a program needn't handle non-finite values.
Results may differ from a plain program's by a relative error of at most 0.038.
Values may be sent and summed in bfloat16 or wider, within the bound.
No kernel may reach another device: no remote copies, remote signals or barrier semaphores. Data moves between devices by JAX's collectives and lax.ppermute only.
A program may use at most 128 MiB of HBM per device.

v0:
```python
import jax
import jax.numpy as jnp
from jax import lax
from jax.sharding import PartitionSpec as P

HD = 128


def from_behind(value, axis, steps):
    count = lax.axis_size(axis)
    pairs = [(source, (source + steps) % count) for source in range(count)]
    return lax.ppermute(value, axis, pairs)


def row_positions(block_order, first_row, number, half):
    row_ids = first_row + jnp.arange(number, dtype=jnp.int32)
    owners = row_ids // half
    slots = jnp.arange(block_order.shape[0], dtype=jnp.int32)
    picked = jnp.sum(jnp.where(owners[:, None] == slots[None, :], block_order[None, :], 0), axis=1)
    return picked * half + row_ids % half


def document_of(positions, limits):
    return jnp.sum((positions[:, None] >= limits[None, :]).astype(jnp.int32), axis=1)


def visible(query_pos, query_doc, key_pos, key_doc):
    return (key_pos[None, :] <= query_pos[:, None]) & (key_doc[None, :] == query_doc[:, None])


def tile_scores(query_heads, key_heads, allowed, factor):
    scores = (
        jnp.einsum("qhd,khd->hqk", query_heads, key_heads, preferred_element_type=jnp.float32)
        * factor
    )
    return jnp.where(allowed[None], scores, -1e30)


def tile_grads(query_heads, outer_heads, log_norm, delta, key_heads, value_heads, allowed, factor):
    scores = tile_scores(query_heads, key_heads, allowed, factor)
    weights = jnp.where(allowed[None], jnp.exp(scores - log_norm[:, :, None]), 0.0)
    weight_grad = jnp.einsum(
        "qhd,khd->hqk", outer_heads, value_heads, preferred_element_type=jnp.float32
    )
    score_grad = (weights * (weight_grad - delta[:, :, None]) * factor).astype(jnp.bfloat16)
    return (weights.astype(jnp.bfloat16), score_grad)


def rank_total(partials):
    summed = lax.psum(partials, "head")
    return tuple((item.astype(jnp.bfloat16) for item in summed))


def local(
    query,
    keys,
    values,
    out_grad,
    gate_left,
    up_left,
    gate_right,
    up_right,
    down_left,
    down_right,
    block_order,
    doc_lengths,
):
    local_rows, local_width = query.shape
    local_heads = local_width // HD
    factor = HD ** (-0.5)
    half = local_rows // 2
    cycle_size = lax.axis_size("ctx")
    position_me = lax.axis_index("ctx")
    limits = jnp.cumsum(doc_lengths)
    own_pos = row_positions(block_order, position_me * local_rows, local_rows, half)
    own_doc = document_of(own_pos, limits)
    query_heads = query.reshape(local_rows, local_heads, HD)
    piece = lax.all_gather(keys, "ctx", axis=0, tiled=True)
    highest = jnp.full((local_heads, local_rows), -1e30, jnp.float32)
    number = piece.shape[0]
    piece_pos = row_positions(block_order, jnp.int32(0), number, half)
    allowed = visible(own_pos, own_doc, piece_pos, document_of(piece_pos, limits))
    scores = tile_scores(query_heads, piece.reshape(number, local_heads, HD), allowed, factor)
    new_high = jnp.maximum(highest, jnp.max(scores, axis=2))
    weights = jnp.where(allowed[None], jnp.exp(scores - new_high[:, :, None]), 0.0)
    totals = jnp.sum(weights, axis=2)
    highest, totals = (new_high, totals)
    log_norm = highest + jnp.log(totals)
    key_piece = lax.all_gather(keys, "ctx", axis=0, tiled=True)
    value_piece = lax.all_gather(values, "ctx", axis=0, tiled=True)
    number = key_piece.shape[0]
    piece_pos = row_positions(block_order, jnp.int32(0), number, half)
    allowed = visible(own_pos, own_doc, piece_pos, document_of(piece_pos, limits))
    scores = tile_scores(query_heads, key_piece.reshape(number, local_heads, HD), allowed, factor)
    weights = jnp.where(allowed[None], jnp.exp(scores - log_norm[:, :, None]), 0.0).astype(
        jnp.bfloat16
    )
    accum = jnp.einsum(
        "hqk,khd->hqd",
        weights,
        value_piece.reshape(number, local_heads, HD),
        preferred_element_type=jnp.float32,
    )
    attended = jnp.transpose(accum, (1, 0, 2)).reshape(local_rows, local_width).astype(jnp.bfloat16)
    gate_low, up_low = rank_total(
        (
            jnp.dot(attended, gate_left, preferred_element_type=jnp.float32),
            jnp.dot(attended, up_left, preferred_element_type=jnp.float32),
        )
    )
    gate = jnp.dot(gate_low, gate_right, preferred_element_type=jnp.float32)
    upval = jnp.dot(up_low, up_right, preferred_element_type=jnp.float32)
    sigma = jax.nn.sigmoid(gate)
    hidden = (gate * sigma * upval).astype(jnp.bfloat16)
    (down_low,) = rank_total((jnp.dot(hidden, down_left, preferred_element_type=jnp.float32),))
    term_down_right = jnp.dot(down_low.T, out_grad, preferred_element_type=jnp.float32)
    (grad_down,) = rank_total(
        (jnp.dot(out_grad, down_right.T, preferred_element_type=jnp.float32),)
    )
    grad_hidden = jnp.dot(grad_down, down_left.T, preferred_element_type=jnp.float32)
    term_down_left = jnp.dot(hidden.T, grad_down, preferred_element_type=jnp.float32)
    grad_gate = (grad_hidden * upval * sigma * (1.0 + gate * (1.0 - sigma))).astype(jnp.bfloat16)
    grad_up = (grad_hidden * gate * sigma).astype(jnp.bfloat16)
    term_gate_right = jnp.dot(gate_low.T, grad_gate, preferred_element_type=jnp.float32)
    term_up_right = jnp.dot(up_low.T, grad_up, preferred_element_type=jnp.float32)
    grad_gate_low, grad_up_low = rank_total(
        (
            jnp.dot(grad_gate, gate_right.T, preferred_element_type=jnp.float32),
            jnp.dot(grad_up, up_right.T, preferred_element_type=jnp.float32),
        )
    )
    term_gate_left = jnp.dot(attended.T, grad_gate_low, preferred_element_type=jnp.float32)
    term_up_left = jnp.dot(attended.T, grad_up_low, preferred_element_type=jnp.float32)
    grad_attended = (
        out_grad.astype(jnp.float32)
        + jnp.dot(grad_gate_low, gate_left.T, preferred_element_type=jnp.float32)
        + jnp.dot(grad_up_low, up_left.T, preferred_element_type=jnp.float32)
    ).astype(jnp.bfloat16)
    grad_gate_left, grad_up_left, grad_down_left = (
        lax.psum_scatter(
            term_gate_left.astype(jnp.bfloat16), "ctx", scatter_dimension=1, tiled=True
        ).astype(jnp.float32),
        lax.psum_scatter(
            term_up_left.astype(jnp.bfloat16), "ctx", scatter_dimension=1, tiled=True
        ).astype(jnp.float32),
        lax.psum_scatter(
            term_down_left.astype(jnp.bfloat16), "ctx", scatter_dimension=1, tiled=True
        ).astype(jnp.float32),
    )
    grad_gate_right, grad_up_right, grad_down_right = (
        lax.psum_scatter(
            term_gate_right.astype(jnp.bfloat16), "ctx", scatter_dimension=0, tiled=True
        ).astype(jnp.float32),
        lax.psum_scatter(
            term_up_right.astype(jnp.bfloat16), "ctx", scatter_dimension=0, tiled=True
        ).astype(jnp.float32),
        lax.psum_scatter(
            term_down_right.astype(jnp.bfloat16), "ctx", scatter_dimension=0, tiled=True
        ).astype(jnp.float32),
    )
    outer_heads = grad_attended.reshape(local_rows, local_heads, HD)
    delta = jnp.transpose(
        jnp.sum(
            outer_heads.astype(jnp.float32)
            * attended.reshape(local_rows, local_heads, HD).astype(jnp.float32),
            axis=2,
        )
    )
    zero_heads = jnp.zeros((local_rows, local_heads, HD), jnp.float32)

    def one_turn(turn_number, carried):
        key_now, value_now, key_grad, value_grad, query_grad = carried
        anchor = (position_me - turn_number) % cycle_size
        piece_pos = row_positions(block_order, anchor * local_rows, local_rows, half)
        allowed = visible(own_pos, own_doc, piece_pos, document_of(piece_pos, limits))
        key_now_heads = key_now.reshape(local_rows, local_heads, HD)
        value_now_heads = value_now.reshape(local_rows, local_heads, HD)
        weights, score_grad = tile_grads(
            query_heads,
            outer_heads,
            log_norm,
            delta,
            key_now_heads,
            value_now_heads,
            allowed,
            factor,
        )
        query_grad = query_grad + jnp.einsum(
            "hqk,khd->qhd", score_grad, key_now_heads, preferred_element_type=jnp.float32
        )
        key_grad = key_grad + jnp.einsum(
            "hqk,qhd->khd", score_grad, query_heads, preferred_element_type=jnp.float32
        )
        value_grad = value_grad + jnp.einsum(
            "hqk,qhd->khd", weights, outer_heads, preferred_element_type=jnp.float32
        )
        key_now, value_now = from_behind((key_now, value_now), "ctx", 1)
        key_grad, value_grad = from_behind((key_grad, value_grad), "ctx", 1)
        return (key_now, value_now, key_grad, value_grad, query_grad)

    final_state = lax.fori_loop(
        0, cycle_size, one_turn, (keys, values, zero_heads, zero_heads, zero_heads)
    )
    key_grad, value_grad, query_grad = (final_state[2], final_state[3], final_state[4])
    grad_query = query_grad.reshape(local_rows, local_width).astype(jnp.bfloat16)
    grad_keys = key_grad.reshape(local_rows, local_width).astype(jnp.bfloat16)
    grad_values = value_grad.reshape(local_rows, local_width).astype(jnp.bfloat16)
    return (
        grad_query,
        grad_keys,
        grad_values,
        grad_gate_left,
        grad_up_left,
        grad_down_left,
        grad_gate_right,
        grad_up_right,
        grad_down_right,
    )


def solution(mesh):
    in_specs = (
        P("ctx", "head"),
        P("ctx", "head"),
        P("ctx", "head"),
        P("ctx", "head"),
        P("head", None),
        P("head", None),
        P(None, "head"),
        P(None, "head"),
        P("head", None),
        P(None, "head"),
        P(),
        P(),
    )
    out_specs = (
        P("ctx", "head"),
        P("ctx", "head"),
        P("ctx", "head"),
        P("head", "ctx"),
        P("head", "ctx"),
        P("head", "ctx"),
        P("ctx", "head"),
        P("ctx", "head"),
        P("ctx", "head"),
    )
    return jax.shard_map(local, mesh=mesh, in_specs=in_specs, out_specs=out_specs, check_vma=False)
```

profile of v0, /device:TPU:4, one launch (start us, length us, event | category | flops | bytes accessed | tf_op | source)
XLA Modules:
  0.0 700.6 jit_solution(6445927343042173931)
XLA Ops:
  17.3 35.9 %all-gather.3.cloned.1.call-done = bf16[4096,256]{0,1:T(8,128)(2,1)} async-done(((bf16[256,256]{0,1:T(8,128)(2,1)}), bf16[4096,256]{0,1:T(8,128)(2,1)}) %all-gather.3.cloned.1.call-update) | async-done | bytes 2097168 | tf_op jit(solution)/shard_map/all_gather | solution.py:78
  53.2 3.8 fusion.50
  57.0 2.1 select_reduce_fusion.1
  60.2 32.1 %all-gather.5.cloned.1.call-done = bf16[4096,256]{1,0:T(8,128)(2,1)} async-done(((bf16[256,256]{1,0:T(8,128)(2,1)}), bf16[4096,256]{1,0:T(8,128)(2,1)}) %all-gather.5.cloned.1.call-update) | async-done | bytes 2097168 | tf_op jit(solution)/shard_map/all_gather | solution.py:90
  92.4 4.1 copy.58
  96.5 5.8 fusion.24
  104.4 98.6 %all-reduce.4 = (bf16[256,512]{1,0:T(8,128)(2,1)S(1)}, bf16[256,512]{1,0:T(8,128)(2,1)S(1)}, bf16[256,512]{1,0:T(8,128)(2,1)}) all-reduce(f32[256,512]{1,0:T(8,128)} %fusion.53, f32[256,512]{1,0:T(8,128)S(1)} %fusion.51, f32[256,512]{1,0:T(8,128)} %fusion.52), channel_id=1, replica_groups=mesh['ctx'=16,'head'=16] {'head'}, use_global_device_ids=true, to_apply=%region_9.10 | all-reduce | flops 393216 | bytes 2359296 | tf_op jit(solution)/shard_map/psum | solution.py:50
  206.8 97.0 %all-reduce.5 = (bf16[256,512]{1,0:T(8,128)(2,1)S(1)}, bf16[256,512]{1,0:T(8,128)(2,1)}, bf16[256,512]{1,0:T(8,128)(2,1)}) all-reduce(f32[256,512]{1,0:T(8,128)S(1)} %fusion.54, f32[256,512]{1,0:T(8,128)S(1)} %fusion.55, f32[256,512]{1,0:T(8,128)S(1)} %fusion.56), channel_id=1, replica_groups=mesh['ctx'=16,'head'=16] {'head'}, use_global_device_ids=true, to_apply=%region_10.11 | all-reduce | flops 393216 | bytes 2359296 | tf_op jit(solution)/shard_map/psum | solution.py:50
  303.7 2.0 convolution_convert_fusion.4
  306.9 2.0 convolution_convert_fusion.3
  309.2 2.4 convolution_convert_fusion
  311.6 2.3 convolution_convert_fusion.1
  317.3 246.3 %while.25 = (s32[]{:T(128)}, bf16[256,256]{1,0:T(8,128)(2,1)S(1)}, bf16[256,256]{1,0:T(8,128)(2,1)S(1)}, f32[256,2,128]{2,0,1:T(8,128)S(1)}, f32[256,2,128]{2,0,...) while((s32[]{:T(128)}, bf16[256,256]{1,0:T(8,128)(2,1)S(1)}, ...), condition=%wide.region_16.17_spmd.clone, body=%wide.region_13.16_spmd.clone.sunk | while | flops 169445392 | bytes 8666748 | solution.py:201
  318.9 2.6 collective-permute-start.3
  322.3 8.9 %collective-permute-done = bf16[256,256]{1,0:T(8,128)(2,1)S(1)} collective-permute-done((bf16[256,256]{1,0:T(8,128)(2,1)S(1)}, bf16[256,256]{1,0:T(8,128)(2,1)S(1)}, u32[]{:S(2)}, u32[]{:S(2)}) %collective-permute-start) | collective-permute-done | bytes 131104 | tf_op jit(solution)/shard_map/while/body/eval_jaxpr/ppermute | solution.py:12
  336.4 9.9 %collective-permute-done = bf16[256,256]{1,0:T(8,128)(2,1)S(1)} collective-permute-done((bf16[256,256]{1,0:T(8,128)(2,1)S(1)}, bf16[256,256]{1,0:T(8,128)(2,1)S(1)}, u32[]{:S(2)}, u32[]{:S(2)}) %collective-permute-start) | collective-permute-done | bytes 131104 | tf_op jit(solution)/shard_map/while/body/eval_jaxpr/ppermute | solution.py:12
  350.4 11.2 %collective-permute-done = bf16[256,256]{1,0:T(8,128)(2,1)S(1)} collective-permute-done((bf16[256,256]{1,0:T(8,128)(2,1)S(1)}, bf16[256,256]{1,0:T(8,128)(2,1)S(1)}, u32[]{:S(2)}, u32[]{:S(2)}) %collective-permute-start) | collective-permute-done | bytes 131104 | tf_op jit(solution)/shard_map/while/body/eval_jaxpr/ppermute | solution.py:12
  365.3 11.3 %collective-permute-done = bf16[256,256]{1,0:T(8,128)(2,1)S(1)} collective-permute-done((bf16[256,256]{1,0:T(8,128)(2,1)S(1)}, bf16[256,256]{1,0:T(8,128)(2,1)S(1)}, u32[]{:S(2)}, u32[]{:S(2)}) %collective-permute-start) | collective-permute-done | bytes 131104 | tf_op jit(solution)/shard_map/while/body/eval_jaxpr/ppermute | solution.py:12
  380.1 11.8 %collective-permute-done = bf16[256,256]{1,0:T(8,128)(2,1)S(1)} collective-permute-done((bf16[256,256]{1,0:T(8,128)(2,1)S(1)}, bf16[256,256]{1,0:T(8,128)(2,1)S(1)}, u32[]{:S(2)}, u32[]{:S(2)}) %collective-permute-start) | collective-permute-done | bytes 131104 | tf_op jit(solution)/shard_map/while/body/eval_jaxpr/ppermute | solution.py:12
  395.5 11.7 %collective-permute-done = bf16[256,256]{1,0:T(8,128)(2,1)S(1)} collective-permute-done((bf16[256,256]{1,0:T(8,128)(2,1)S(1)}, bf16[256,256]{1,0:T(8,128)(2,1)S(1)}, u32[]{:S(2)}, u32[]{:S(2)}) %collective-permute-start) | collective-permute-done | bytes 131104 | tf_op jit(solution)/shard_map/while/body/eval_jaxpr/ppermute | solution.py:12
  410.8 11.7 %collective-permute-done = bf16[256,256]{1,0:T(8,128)(2,1)S(1)} collective-permute-done((bf16[256,256]{1,0:T(8,128)(2,1)S(1)}, bf16[256,256]{1,0:T(8,128)(2,1)S(1)}, u32[]{:S(2)}, u32[]{:S(2)}) %collective-permute-start) | collective-permute-done | bytes 131104 | tf_op jit(solution)/shard_map/while/body/eval_jaxpr/ppermute | solution.py:12
  426.0 11.4 %collective-permute-done = bf16[256,256]{1,0:T(8,128)(2,1)S(1)} collective-permute-done((bf16[256,256]{1,0:T(8,128)(2,1)S(1)}, bf16[256,256]{1,0:T(8,128)(2,1)S(1)}, u32[]{:S(2)}, u32[]{:S(2)}) %collective-permute-start) | collective-permute-done | bytes 131104 | tf_op jit(solution)/shard_map/while/body/eval_jaxpr/ppermute | solution.py:12
  440.9 11.6 %collective-permute-done = bf16[256,256]{1,0:T(8,128)(2,1)S(1)} collective-permute-done((bf16[256,256]{1,0:T(8,128)(2,1)S(1)}, bf16[256,256]{1,0:T(8,128)(2,1)S(1)}, u32[]{:S(2)}, u32[]{:S(2)}) %collective-permute-start) | collective-permute-done | bytes 131104 | tf_op jit(solution)/shard_map/while/body/eval_jaxpr/ppermute | solution.py:12
  456.1 11.6 %collective-permute-done = bf16[256,256]{1,0:T(8,128)(2,1)S(1)} collective-permute-done((bf16[256,256]{1,0:T(8,128)(2,1)S(1)}, bf16[256,256]{1,0:T(8,128)(2,1)S(1)}, u32[]{:S(2)}, u32[]{:S(2)}) %collective-permute-start) | collective-permute-done | bytes 131104 | tf_op jit(solution)/shard_map/while/body/eval_jaxpr/ppermute | solution.py:12
  471.2 11.7 %collective-permute-done = bf16[256,256]{1,0:T(8,128)(2,1)S(1)} collective-permute-done((bf16[256,256]{1,0:T(8,128)(2,1)S(1)}, bf16[256,256]{1,0:T(8,128)(2,1)S(1)}, u32[]{:S(2)}, u32[]{:S(2)}) %collective-permute-start) | collective-permute-done | bytes 131104 | tf_op jit(solution)/shard_map/while/body/eval_jaxpr/ppermute | solution.py:12
  486.5 11.6 %collective-permute-done = bf16[256,256]{1,0:T(8,128)(2,1)S(1)} collective-permute-done((bf16[256,256]{1,0:T(8,128)(2,1)S(1)}, bf16[256,256]{1,0:T(8,128)(2,1)S(1)}, u32[]{:S(2)}, u32[]{:S(2)}) %collective-permute-start) | collective-permute-done | bytes 131104 | tf_op jit(solution)/shard_map/while/body/eval_jaxpr/ppermute | solution.py:12
  501.6 11.3 %collective-permute-done = bf16[256,256]{1,0:T(8,128)(2,1)S(1)} collective-permute-done((bf16[256,256]{1,0:T(8,128)(2,1)S(1)}, bf16[256,256]{1,0:T(8,128)(2,1)S(1)}, u32[]{:S(2)}, u32[]{:S(2)}) %collective-permute-start) | collective-permute-done | bytes 131104 | tf_op jit(solution)/shard_map/while/body/eval_jaxpr/ppermute | solution.py:12
  517.0 12.8 %collective-permute-done = bf16[256,256]{1,0:T(8,128)(2,1)S(1)} collective-permute-done((bf16[256,256]{1,0:T(8,128)(2,1)S(1)}, bf16[256,256]{1,0:T(8,128)(2,1)S(1)}, u32[]{:S(2)}, u32[]{:S(2)}) %collective-permute-start) | collective-permute-done | bytes 131104 | tf_op jit(solution)/shard_map/while/body/eval_jaxpr/ppermute | solution.py:12
  533.6 12.5 %collective-permute-done = bf16[256,256]{1,0:T(8,128)(2,1)S(1)} collective-permute-done((bf16[256,256]{1,0:T(8,128)(2,1)S(1)}, bf16[256,256]{1,0:T(8,128)(2,1)S(1)}, u32[]{:S(2)}, u32[]{:S(2)}) %collective-permute-start) | collective-permute-done | bytes 131104 | tf_op jit(solution)/shard_map/while/body/eval_jaxpr/ppermute | solution.py:12
  549.6 12.6 %collective-permute-done = bf16[256,256]{1,0:T(8,128)(2,1)S(1)} collective-permute-done((bf16[256,256]{1,0:T(8,128)(2,1)S(1)}, bf16[256,256]{1,0:T(8,128)(2,1)S(1)}, u32[]{:S(2)}, u32[]{:S(2)}) %collective-permute-start) | collective-permute-done | bytes 131104 | tf_op jit(solution)/shard_map/while/body/eval_jaxpr/ppermute | solution.py:12
  571.1 56.5 %reduce-scatter.13.cloned.1.call-done = bf16[32,688]{1,0:T(8,128)(2,1)} async-done(((bf16[512,688]{1,0:T(8,128)(2,1)}), bf16[32,688]{1,0:T(8,128)(2,1)}) %reduce-scatter.13.cloned.1.call-update) | async-done | bytes 44048 | tf_op jit(solution)/shard_map/reduce_scatter | solution.py:151
  629.0 63.3 %reduce-scatter.11.cloned.1.call-done = bf16[688,32]{0,1:T(8,128)(2,1)} async-done(((bf16[688,512]{0,1:T(8,128)(2,1)}), bf16[688,32]{0,1:T(8,128)(2,1)}) %reduce-scatter.11.cloned.1.call-update) | async-done | bytes 44048 | tf_op jit(solution)/shard_map/reduce_scatter | solution.py:146
  (414 shorter events, 90.7 us)
Async XLA Ops:
  7.2 46.0 %all-gather.3.cloned.1.call-start = ((), (), s32[]{:S(2)}) async-start(), calls=%async_computation.6 | async-start | bytes 2228224 | tf_op jit(solution)/shard_map/all_gather | solution.py:78
  10.6 81.8 %all-gather.5.cloned.1.call-start = ((), (), s32[]{:S(2)}) async-start(), calls=%async_computation.7 | async-start | bytes 2228224 | tf_op jit(solution)/shard_map/all_gather | solution.py:90
  11.3 554.3 %reduce-scatter.9.cloned.1.call-start = ((), (), s32[]{:S(2)}) async-start(), calls=%async_computation.9 | async-start | bytes 278528 | tf_op jit(solution)/shard_map/reduce_scatter | solution.py:143
  305.8 261.2 %reduce-scatter.7.cloned.1.call-start = ((), (), s32[]{:S(2)}) async-start(), calls=%async_computation.8 | async-start | bytes 278528 | tf_op jit(solution)/shard_map/reduce_scatter | solution.py:140
  306.9 261.5 %reduce-scatter.17.cloned.1.call-start = ((), (), s32[]{:S(2)}) async-start(), calls=%async_computation.13 | async-start | bytes 278528 | tf_op jit(solution)/shard_map/reduce_scatter | solution.py:157
  308.9 260.7 %reduce-scatter.15.cloned.1.call-start = ((), (), s32[]{:S(2)}) async-start(), calls=%async_computation.12 | async-start | bytes 835584 | tf_op jit(solution)/shard_map/reduce_scatter | solution.py:154
  311.6 316.0 %reduce-scatter.13.cloned.1.call-start = ((), (), s32[]{:S(2)}) async-start(), calls=%async_computation.11 | async-start | bytes 835584 | tf_op jit(solution)/shard_map/reduce_scatter | solution.py:151
  313.9 378.4 %reduce-scatter.11.cloned.1.call-start = ((), (), s32[]{:S(2)}) async-start(), calls=%async_computation.10 | async-start | bytes 835584 | tf_op jit(solution)/shard_map/reduce_scatter | solution.py:146
  318.5 14.0 %collective-permute-start.2 = (f32[256,2,128]{2,0,1:T(8,128)S(1)}, f32[256,2,128]{2,0,1:T(8,128)S(1)}, u32[]{:S(2)}, u32[]{:S(2)}) collective-permute-start(f32[256,2,128]{2,0,1:T(8,128)S(1)} %fusion.140), channel_id=1, source_target_pairs={{0,16},{16,32},{32,48},{48,64},{64,80},{80,96},{96,112},{112,128},... | collective-permute-start | bytes 786440 | tf_op jit(solution)/shard_map/while/body/eval_jaxpr/ppermute | solution.py:12
  333.8 14.0 %collective-permute-start.2 = (f32[256,2,128]{2,0,1:T(8,128)S(1)}, f32[256,2,128]{2,0,1:T(8,128)S(1)}, u32[]{:S(2)}, u32[]{:S(2)}) collective-permute-start(f32[256,2,128]{2,0,1:T(8,128)S(1)} %fusion.140), channel_id=1, source_target_pairs={{0,16},{16,32},{32,48},{48,64},{64,80},{80,96},{96,112},{112,128},... | collective-permute-start | bytes 786440 | tf_op jit(solution)/shard_map/while/body/eval_jaxpr/ppermute | solution.py:12
  349.0 14.1 %collective-permute-start.2 = (f32[256,2,128]{2,0,1:T(8,128)S(1)}, f32[256,2,128]{2,0,1:T(8,128)S(1)}, u32[]{:S(2)}, u32[]{:S(2)}) collective-permute-start(f32[256,2,128]{2,0,1:T(8,128)S(1)} %fusion.140), channel_id=1, source_target_pairs={{0,16},{16,32},{32,48},{48,64},{64,80},{80,96},{96,112},{112,128},... | collective-permute-start | bytes 786440 | tf_op jit(solution)/shard_map/while/body/eval_jaxpr/ppermute | solution.py:12
  349.4 13.8 %collective-permute-start.3 = (f32[256,2,128]{2,0,1:T(8,128)S(1)}, f32[256,2,128]{2,0,1:T(8,128)S(1)}, u32[]{:S(2)}, u32[]{:S(2)}) collective-permute-start(f32[256,2,128]{2,0,1:T(8,128)S(1)} %fusion.141), channel_id=1, source_target_pairs={{0,16},{16,32},{32,48},{48,64},{64,80},{80,96},{96,112},{112,128},... | collective-permute-start | bytes 786440 | tf_op jit(solution)/shard_map/while/body/eval_jaxpr/ppermute | solution.py:12
  379.2 14.2 %collective-permute-start.2 = (f32[256,2,128]{2,0,1:T(8,128)S(1)}, f32[256,2,128]{2,0,1:T(8,128)S(1)}, u32[]{:S(2)}, u32[]{:S(2)}) collective-permute-start(f32[256,2,128]{2,0,1:T(8,128)S(1)} %fusion.140), channel_id=1, source_target_pairs={{0,16},{16,32},{32,48},{48,64},{64,80},{80,96},{96,112},{112,128},... | collective-permute-start | bytes 786440 | tf_op jit(solution)/shard_map/while/body/eval_jaxpr/ppermute | solution.py:12
  379.5 13.8 %collective-permute-start.3 = (f32[256,2,128]{2,0,1:T(8,128)S(1)}, f32[256,2,128]{2,0,1:T(8,128)S(1)}, u32[]{:S(2)}, u32[]{:S(2)}) collective-permute-start(f32[256,2,128]{2,0,1:T(8,128)S(1)} %fusion.141), channel_id=1, source_target_pairs={{0,16},{16,32},{32,48},{48,64},{64,80},{80,96},{96,112},{112,128},... | collective-permute-start | bytes 786440 | tf_op jit(solution)/shard_map/while/body/eval_jaxpr/ppermute | solution.py:12
  394.6 14.1 %collective-permute-start.2 = (f32[256,2,128]{2,0,1:T(8,128)S(1)}, f32[256,2,128]{2,0,1:T(8,128)S(1)}, u32[]{:S(2)}, u32[]{:S(2)}) collective-permute-start(f32[256,2,128]{2,0,1:T(8,128)S(1)} %fusion.140), channel_id=1, source_target_pairs={{0,16},{16,32},{32,48},{48,64},{64,80},{80,96},{96,112},{112,128},... | collective-permute-start | bytes 786440 | tf_op jit(solution)/shard_map/while/body/eval_jaxpr/ppermute | solution.py:12
  394.9 13.8 %collective-permute-start.3 = (f32[256,2,128]{2,0,1:T(8,128)S(1)}, f32[256,2,128]{2,0,1:T(8,128)S(1)}, u32[]{:S(2)}, u32[]{:S(2)}) collective-permute-start(f32[256,2,128]{2,0,1:T(8,128)S(1)} %fusion.141), channel_id=1, source_target_pairs={{0,16},{16,32},{32,48},{48,64},{64,80},{80,96},{96,112},{112,128},... | collective-permute-start | bytes 786440 | tf_op jit(solution)/shard_map/while/body/eval_jaxpr/ppermute | solution.py:12
  409.9 14.0 %collective-permute-start.2 = (f32[256,2,128]{2,0,1:T(8,128)S(1)}, f32[256,2,128]{2,0,1:T(8,128)S(1)}, u32[]{:S(2)}, u32[]{:S(2)}) collective-permute-start(f32[256,2,128]{2,0,1:T(8,128)S(1)} %fusion.140), channel_id=1, source_target_pairs={{0,16},{16,32},{32,48},{48,64},{64,80},{80,96},{96,112},{112,128},... | collective-permute-start | bytes 786440 | tf_op jit(solution)/shard_map/while/body/eval_jaxpr/ppermute | solution.py:12
  440.0 14.0 %collective-permute-start.2 = (f32[256,2,128]{2,0,1:T(8,128)S(1)}, f32[256,2,128]{2,0,1:T(8,128)S(1)}, u32[]{:S(2)}, u32[]{:S(2)}) collective-permute-start(f32[256,2,128]{2,0,1:T(8,128)S(1)} %fusion.140), channel_id=1, source_target_pairs={{0,16},{16,32},{32,48},{48,64},{64,80},{80,96},{96,112},{112,128},... | collective-permute-start | bytes 786440 | tf_op jit(solution)/shard_map/while/body/eval_jaxpr/ppermute | solution.py:12
  455.1 14.0 %collective-permute-start.2 = (f32[256,2,128]{2,0,1:T(8,128)S(1)}, f32[256,2,128]{2,0,1:T(8,128)S(1)}, u32[]{:S(2)}, u32[]{:S(2)}) collective-permute-start(f32[256,2,128]{2,0,1:T(8,128)S(1)} %fusion.140), channel_id=1, source_target_pairs={{0,16},{16,32},{32,48},{48,64},{64,80},{80,96},{96,112},{112,128},... | collective-permute-start | bytes 786440 | tf_op jit(solution)/shard_map/while/body/eval_jaxpr/ppermute | solution.py:12
  470.3 14.1 %collective-permute-start.2 = (f32[256,2,128]{2,0,1:T(8,128)S(1)}, f32[256,2,128]{2,0,1:T(8,128)S(1)}, u32[]{:S(2)}, u32[]{:S(2)}) collective-permute-start(f32[256,2,128]{2,0,1:T(8,128)S(1)} %fusion.140), channel_id=1, source_target_pairs={{0,16},{16,32},{32,48},{48,64},{64,80},{80,96},{96,112},{112,128},... | collective-permute-start | bytes 786440 | tf_op jit(solution)/shard_map/while/body/eval_jaxpr/ppermute | solution.py:12
  485.6 13.9 %collective-permute-start.2 = (f32[256,2,128]{2,0,1:T(8,128)S(1)}, f32[256,2,128]{2,0,1:T(8,128)S(1)}, u32[]{:S(2)}, u32[]{:S(2)}) collective-permute-start(f32[256,2,128]{2,0,1:T(8,128)S(1)} %fusion.140), channel_id=1, source_target_pairs={{0,16},{16,32},{32,48},{48,64},{64,80},{80,96},{96,112},{112,128},... | collective-permute-start | bytes 786440 | tf_op jit(solution)/shard_map/while/body/eval_jaxpr/ppermute | solution.py:12
  500.7 14.1 %collective-permute-start.2 = (f32[256,2,128]{2,0,1:T(8,128)S(1)}, f32[256,2,128]{2,0,1:T(8,128)S(1)}, u32[]{:S(2)}, u32[]{:S(2)}) collective-permute-start(f32[256,2,128]{2,0,1:T(8,128)S(1)} %fusion.140), channel_id=1, source_target_pairs={{0,16},{16,32},{32,48},{48,64},{64,80},{80,96},{96,112},{112,128},... | collective-permute-start | bytes 786440 | tf_op jit(solution)/shard_map/while/body/eval_jaxpr/ppermute | solution.py:12
  501.1 13.8 %collective-permute-start.3 = (f32[256,2,128]{2,0,1:T(8,128)S(1)}, f32[256,2,128]{2,0,1:T(8,128)S(1)}, u32[]{:S(2)}, u32[]{:S(2)}) collective-permute-start(f32[256,2,128]{2,0,1:T(8,128)S(1)} %fusion.141), channel_id=1, source_target_pairs={{0,16},{16,32},{32,48},{48,64},{64,80},{80,96},{96,112},{112,128},... | collective-permute-start | bytes 786440 | tf_op jit(solution)/shard_map/while/body/eval_jaxpr/ppermute | solution.py:12
  516.0 15.4 %collective-permute-start.2 = (f32[256,2,128]{2,0,1:T(8,128)S(1)}, f32[256,2,128]{2,0,1:T(8,128)S(1)}, u32[]{:S(2)}, u32[]{:S(2)}) collective-permute-start(f32[256,2,128]{2,0,1:T(8,128)S(1)} %fusion.140), channel_id=1, source_target_pairs={{0,16},{16,32},{32,48},{48,64},{64,80},{80,96},{96,112},{112,128},... | collective-permute-start | bytes 786440 | tf_op jit(solution)/shard_map/while/body/eval_jaxpr/ppermute | solution.py:12
  516.4 15.1 %collective-permute-start.3 = (f32[256,2,128]{2,0,1:T(8,128)S(1)}, f32[256,2,128]{2,0,1:T(8,128)S(1)}, u32[]{:S(2)}, u32[]{:S(2)}) collective-permute-start(f32[256,2,128]{2,0,1:T(8,128)S(1)} %fusion.141), channel_id=1, source_target_pairs={{0,16},{16,32},{32,48},{48,64},{64,80},{80,96},{96,112},{112,128},... | collective-permute-start | bytes 786440 | tf_op jit(solution)/shard_map/while/body/eval_jaxpr/ppermute | solution.py:12
  516.6 14.9 %collective-permute-start.1 = (bf16[256,256]{1,0:T(8,128)(2,1)S(1)}, bf16[256,256]{1,0:T(8,128)(2,1)S(1)}, u32[]{:S(2)}, u32[]{:S(2)}) collective-permute-start(bf16[256,256]{1,0:T(8,128)(2,1)S(1)} %copy.110), channel_id=1, source_target_pairs={{0,16},{16,32},{32,48},{48,64},{64,80},{80,96},{96,112},{112,128},... | collective-permute-start | bytes 393224 | tf_op jit(solution)/shard_map/while/body/eval_jaxpr/ppermute | solution.py:12
  532.7 14.8 %collective-permute-start.2 = (f32[256,2,128]{2,0,1:T(8,128)S(1)}, f32[256,2,128]{2,0,1:T(8,128)S(1)}, u32[]{:S(2)}, u32[]{:S(2)}) collective-permute-start(f32[256,2,128]{2,0,1:T(8,128)S(1)} %fusion.140), channel_id=1, source_target_pairs={{0,16},{16,32},{32,48},{48,64},{64,80},{80,96},{96,112},{112,128},... | collective-permute-start | bytes 786440 | tf_op jit(solution)/shard_map/while/body/eval_jaxpr/ppermute | solution.py:12
  533.0 14.4 %collective-permute-start.3 = (f32[256,2,128]{2,0,1:T(8,128)S(1)}, f32[256,2,128]{2,0,1:T(8,128)S(1)}, u32[]{:S(2)}, u32[]{:S(2)}) collective-permute-start(f32[256,2,128]{2,0,1:T(8,128)S(1)} %fusion.141), channel_id=1, source_target_pairs={{0,16},{16,32},{32,48},{48,64},{64,80},{80,96},{96,112},{112,128},... | collective-permute-start | bytes 786440 | tf_op jit(solution)/shard_map/while/body/eval_jaxpr/ppermute | solution.py:12
  533.2 14.2 %collective-permute-start.1 = (bf16[256,256]{1,0:T(8,128)(2,1)S(1)}, bf16[256,256]{1,0:T(8,128)(2,1)S(1)}, u32[]{:S(2)}, u32[]{:S(2)}) collective-permute-start(bf16[256,256]{1,0:T(8,128)(2,1)S(1)} %copy.110), channel_id=1, source_target_pairs={{0,16},{16,32},{32,48},{48,64},{64,80},{80,96},{96,112},{112,128},... | collective-permute-start | bytes 393224 | tf_op jit(solution)/shard_map/while/body/eval_jaxpr/ppermute | solution.py:12
  548.7 14.9 %collective-permute-start.2 = (f32[256,2,128]{2,0,1:T(8,128)S(1)}, f32[256,2,128]{2,0,1:T(8,128)S(1)}, u32[]{:S(2)}, u32[]{:S(2)}) collective-permute-start(f32[256,2,128]{2,0,1:T(8,128)S(1)} %fusion.140), channel_id=1, source_target_pairs={{0,16},{16,32},{32,48},{48,64},{64,80},{80,96},{96,112},{112,128},... | collective-permute-start | bytes 786440 | tf_op jit(solution)/shard_map/while/body/eval_jaxpr/ppermute | solution.py:12
  549.0 14.5 %collective-permute-start.3 = (f32[256,2,128]{2,0,1:T(8,128)S(1)}, f32[256,2,128]{2,0,1:T(8,128)S(1)}, u32[]{:S(2)}, u32[]{:S(2)}) collective-permute-start(f32[256,2,128]{2,0,1:T(8,128)S(1)} %fusion.141), channel_id=1, source_target_pairs={{0,16},{16,32},{32,48},{48,64},{64,80},{80,96},{96,112},{112,128},... | collective-permute-start | bytes 786440 | tf_op jit(solution)/shard_map/while/body/eval_jaxpr/ppermute | solution.py:12
  549.2 14.4 %collective-permute-start.1 = (bf16[256,256]{1,0:T(8,128)(2,1)S(1)}, bf16[256,256]{1,0:T(8,128)(2,1)S(1)}, u32[]{:S(2)}, u32[]{:S(2)}) collective-permute-start(bf16[256,256]{1,0:T(8,128)(2,1)S(1)} %copy.110), channel_id=1, source_target_pairs={{0,16},{16,32},{32,48},{48,64},{64,80},{80,96},{96,112},{112,128},... | collective-permute-start | bytes 393224 | tf_op jit(solution)/shard_map/while/body/eval_jaxpr/ppermute | solution.py:12
  (63 other events, 1261.3 us)
Sparse Core Ops, SparseCore 0:
  10.7 42.4 all-gather.2
  55.6 36.6 all-gather.4
  305.9 62.4 reduce-scatter.8
  370.9 61.8 reduce-scatter.6
  435.2 61.9 reduce-scatter.16
  499.7 63.2 reduce-scatter.14
  565.5 62.0 reduce-scatter.12
  630.3 62.0 reduce-scatter.10
where the time goes:
time: 702 us; the launch traced here: 701 us
  waiting for transfers between devices  396 us (56%)
  blocking collectives  196 us (28%)
  matrix products  50.5 us (7%)
  other arithmetic  20.1 us (3%)
  between operations  14.6 us (2%)
  local copies, waits for them, and re-layouts  11.8 us (2%)
  starting transfers between devices  10.7 us (2%)
    ppermute x64, waiting for transfers between devices, from_behind(): return lax.ppermute(value, axis, pairs)  207 us
    psum x2, blocking collectives, rank_total(): summed = lax.psum(partials, 'head')  196 us
    reduce_scatter x1, waiting for transfers between devices, local(): lax.psum_scatter(term_down_left.astype(jnp.bfloat16), 'ctx', scatter_dime...  63.3 us
    reduce_scatter x1, waiting for transfers between devices, local(): lax.psum_scatter(term_gate_right.astype(jnp.bfloat16), 'ctx', scatter_dim...  56.5 us
    all_gather x1, waiting for transfers between devices, local(): piece = lax.all_gather(keys, 'ctx', axis=0, tiled=True)  35.9 us
    all_gather x1, waiting for transfers between devices, local(): value_piece = lax.all_gather(values, 'ctx', axis=0, tiled=True)  32.1 us
  transfers between devices with their start and end apart: 72, of which 36 were waited for; matrix products, arithmetic and copies ran while one was open for 8% of the time, Pallas kernels for 0%

commit v1 on v0

v1 whole, which is shorter than its diff:
```python
import functools
import math

import jax
import jax.numpy as jnp
from jax import lax
from jax.experimental import pallas as pl
from jax.experimental.pallas import tpu as pltpu
from jax.sharding import PartitionSpec as P

HD = 128
HALF = 128
CHUNK = 4
WIDE = CHUNK * HALF
DOC_BLOCKS = 17
CHUNKS = -(-DOC_BLOCKS // CHUNK)
FACTOR = HD ** (-0.5)
FACTOR2 = FACTOR * math.log2(math.e)
LOW = -1e30
STATS = 16
F32 = jnp.float32
BF16 = jnp.bfloat16
VMEM_BYTES = 32 * 1024 * 1024
GROUP = 16

NT = (((1,), (1,)), ((), ()))
NN = (((1,), (0,)), ((), ()))
TN = (((0,), (0,)), ((), ()))


def mm(left, right, dims):
    return lax.dot_general(left, right, dims, preferred_element_type=F32)


def fill_slots(order_ref, inv_ref):
    for slot in range(order_ref.shape[0]):
        inv_ref[order_ref[slot]] = slot


def doc_edges(lens_ref):
    edges, total = [], jnp.int32(0)
    for number in range(lens_ref.shape[0]):
        total = total + lens_ref[number]
        edges.append(total)
    return edges


def start_of(edges, position):
    start = jnp.zeros_like(position)
    for edge in edges:
        start = jnp.where(edge <= position, edge, start)
    return start


def end_of(edges, position):
    end = jnp.zeros_like(position) + edges[-1]
    for edge in reversed(edges):
        end = jnp.where(edge > position, edge, end)
    return end


def own_slot():
    return lax.axis_index("chip") * 2 + lax.axis_index("core")


def slots_of(inv_ref, first):
    return [
        inv_ref[jnp.minimum(first + turn, inv_ref.shape[0] - 1)] for turn in range(CHUNK)
    ]


def rows_of(ref, slots, cols):
    parts = []
    for slot in slots:
        start = pl.multiple_of((slot % 2) * HALF, HALF)
        parts.append(ref[slot // 4, (slot // 2) % 2, pl.ds(start, HALF), cols])
    return jnp.concatenate(parts, axis=0)


def lane_groups(value, op):
    total = value[:, :HALF]
    for turn in range(1, CHUNK):
        total = op(total, value[:, turn * HALF : (turn + 1) * HALF])
    return total


def query_range(order_ref, edges, half):
    block = order_ref[2 * own_slot() + half]
    first = start_of(edges, block * HALF) // HALF
    turns = (block - first + CHUNK) // CHUNK
    rows = block * HALF + lax.broadcasted_iota(jnp.int32, (HALF, 1), 0)
    return first, turns, rows, start_of(edges, rows)


def key_mask(first, rows, starts):
    lanes = first * HALF + lax.broadcasted_iota(jnp.int32, (HALF, WIDE), 1)
    return (lanes <= rows) & (lanes >= starts)


PLACES = ((0, 0), (3, 0), (1, 0), (0, 1), (3, 1), (1, 1), (2, 0), (2, 1))
PACKED = 4
CTX = ("chip", "core")
BLOCKS = len(PLACES) + 2


def fetch(blocks, all_ref, sems):
    chip, core = lax.axis_index("chip"), lax.axis_index("core")
    row, pair = chip // 2, chip % 2
    rows = blocks[0].shape[0]
    others = [
        pack.at[pl.ds(number * rows, rows)]
        for pack in blocks[len(PLACES) :]
        for number in range(PACKED)
    ]
    copies = []
    for sources, side in ((blocks, core), (others, 1 - core)):
        for (up, across), source in zip(PLACES, sources):
            place = ((row + up) % 4) * 2 + (pair + across) % 2
            copies.append(
                pltpu.make_async_copy(source, all_ref.at[place, side], sems.at[len(copies)])
            )
    for copy in copies:
        copy.start()
    return copies


def fetch_pair(mine_ref, other_ref, all_ref, sems, first):
    core = lax.axis_index("core")
    copies = [
        pltpu.make_async_copy(mine_ref, all_ref.at[:, core], sems.at[first]),
        pltpu.make_async_copy(other_ref, all_ref.at[:, 1 - core], sems.at[first + 1]),
    ]
    for copy in copies:
        copy.start()
    return copies


def settle(copies):
    for copy in copies:
        copy.wait()


def pack_kernel(*refs):
    sources, out_ref = refs[:PACKED], refs[PACKED]
    rows = sources[0].shape[0]
    for number, source in enumerate(sources):
        out_ref[number * rows : (number + 1) * rows] = source[...]


def first_kernel(k_ref, v_ref, og_ref, dr_ref, out_ref, part_ref):
    width = k_ref.shape[1]
    part_ref[...] = mm(og_ref[...], dr_ref[...], NT).astype(BF16)
    for number, source in enumerate((k_ref, v_ref)):
        out_ref[:, number * width : (number + 1) * width] = source[...]


def sum_kernel(*refs):
    out_ref = refs[-1]
    rows = out_ref.shape[0] // GROUP
    base = 0
    for held_ref in refs[:-1]:
        cols = slice(base, base + held_ref.shape[1])
        base = base + held_ref.shape[1]
        total = held_ref[:rows].astype(F32)
        for turn in range(1, GROUP):
            total = total + held_ref[turn * rows : (turn + 1) * rows].astype(F32)
        total = total.astype(BF16)
        for turn in range(GROUP):
            out_ref[turn * rows : (turn + 1) * rows, cols] = total


def cast_kernel(held_ref, *outs):
    rows = outs[0].shape[0]
    for number, out in enumerate(outs):
        out[...] = held_ref[number * rows : (number + 1) * rows].astype(out.dtype)


def token_sum_kernel(held_ref, *outs):
    rows = outs[0].shape[0]
    for number, out in enumerate(outs):
        mine = slice(number * rows, (number + 1) * rows)
        total = held_ref[0, mine].astype(F32)
        for turn in range(1, GROUP):
            total = total + held_ref[turn, mine].astype(F32)
        out[...] = total


def forward_kernel(
    order_ref, lens_ref, q_ref, gl_ref, ul_ref, *refs
):
    blocks, (att_ref, lse_ref, low_ref, inv_ref, s_ref, kv_ref, sems) = refs[:BLOCKS], refs[BLOCKS:]
    copies = fetch(blocks, kv_ref, sems)
    fill_slots(order_ref, inv_ref)
    edges = doc_edges(lens_ref)
    width = q_ref.shape[1]
    heads = width // HD
    settle(copies)
    for half in range(2):
        first, turns, rows, starts = query_range(order_ref, edges, half)
        mine = pl.ds(half * HALF, HALF)

        def score(turn, highs):
            base = first + turn * CHUNK
            keys = rows_of(kv_ref, slots_of(inv_ref, base), slice(0, width))
            ok = key_mask(base, rows, starts)
            out = []
            for head in range(heads):
                cols = slice(head * HD, (head + 1) * HD)
                part = jnp.where(ok, mm(q_ref[mine, cols], keys[:, cols], NT), LOW)
                s_ref[turn, head] = part
                out.append(jnp.maximum(highs[head], lane_groups(part, jnp.maximum)))
            return tuple(out)

        low = jnp.full((HALF, HALF), LOW, F32)
        highs = lax.fori_loop(0, turns, score, (low,) * heads)
        highs = [jnp.max(item, axis=1, keepdims=True) for item in highs]

        def weigh(turn, carried):
            slots = slots_of(inv_ref, first + turn * CHUNK)
            values = rows_of(kv_ref, slots, slice(width, 2 * width))
            out = []
            for head in range(heads):
                cols = slice(head * HD, (head + 1) * HD)
                total, accum = carried[head]
                part = jnp.exp2((s_ref[turn, head] - highs[head]) * FACTOR2)
                total = total + lane_groups(part, jnp.add)
                accum = accum + mm(part.astype(BF16), values[:, cols], NN)
                out.append((total, accum))
            return tuple(out)

        zero = jnp.zeros((HALF, HALF), F32)
        sums = lax.fori_loop(0, turns, weigh, ((zero, zero),) * heads)
        for head in range(heads):
            total = jnp.sum(sums[head][0], axis=1, keepdims=True)
            att_ref[mine, head * HD : (head + 1) * HD] = (sums[head][1] / total).astype(BF16)
            log_norm = highs[head] * FACTOR2 + jnp.log2(total)
            lse_ref[head, mine, :] = jnp.broadcast_to(log_norm, (HALF, HALF))
    rank = gl_ref.shape[1]
    low_ref[:, :rank] = mm(att_ref[...], gl_ref[...], NN).astype(BF16)
    low_ref[:, rank:] = mm(att_ref[...], ul_ref[...], NN).astype(BF16)


def middle_kernel(
    low_ref, grt_ref, urt_ref, dl_ref, back_ref, hidden_ref, gg_ref, gu_ref, mark_ref, acc_ref
):
    rank = dl_ref.shape[1]
    units = dl_ref.shape[0]
    for base in range(0, units, 256):
        cols = slice(base, min(base + 256, units))
        gate = mm(low_ref[:, :rank], grt_ref[cols, :], NT)
        upval = mm(low_ref[:, rank : 2 * rank], urt_ref[cols, :], NT)
        grad_hidden = mm(low_ref[:, 2 * rank :], dl_ref[cols, :], NT)
        sigma = jax.nn.sigmoid(gate)
        silu = gate * sigma
        hidden = (silu * upval).astype(BF16)
        grad_gate = (grad_hidden * upval * sigma * (1.0 + gate * (1.0 - sigma))).astype(BF16)
        grad_up = (grad_hidden * silu).astype(BF16)
        hidden_ref[:, cols] = hidden
        gg_ref[:, cols] = grad_gate
        gu_ref[:, cols] = grad_up
        terms = (
            mm(grad_gate, grt_ref[cols, :], NN),
            mm(grad_up, urt_ref[cols, :], NN),
            mm(hidden, dl_ref[cols, :], NN),
        )
        for number, term in enumerate(terms):
            there = slice(number * rank, (number + 1) * rank)
            if base:
                term = term + acc_ref[:, there]
            if base + 256 >= units:
                back_ref[:, there] = term.astype(BF16)
                mark_ref[...] = term[: mark_ref.shape[0], : mark_ref.shape[1]].astype(BF16)
            else:
                acc_ref[:, there] = term


def outer_terms(pairs, out_ref):
    pieces, height, _ = out_ref.shape
    rows = height // len(pairs)
    step = 256 // rows
    for number, (left, right) in enumerate(pairs):
        for base in range(0, pieces, step):
            term = mm(left[:, base * rows : (base + step) * rows], right[...], TN).astype(BF16)
            for piece in range(step):
                out_ref[base + piece, number * rows : (number + 1) * rows, :] = term[
                    piece * rows : (piece + 1) * rows
                ]


def right_terms_kernel(low_ref, gg_ref, gu_ref, hidden_ref, out_ref):
    rank = low_ref.shape[1] // 3
    pairs = (
        (low_ref.at[:, :rank], gg_ref),
        (low_ref.at[:, rank : 2 * rank], gu_ref),
        (low_ref.at[:, 2 * rank :], hidden_ref),
    )
    outer_terms(pairs, out_ref)


def left_terms_kernel(back_ref, att_ref, og_ref, out_ref):
    rank = back_ref.shape[1] // 3
    pairs = (
        (back_ref.at[:, :rank], att_ref),
        (back_ref.at[:, rank : 2 * rank], att_ref),
        (back_ref.at[:, 2 * rank :], og_ref),
    )
    outer_terms(pairs, out_ref)


def as_rows(column):
    return jnp.transpose(jnp.broadcast_to(column, (HALF, HALF)))[:1]


def split3(value):
    high = value.astype(BF16).astype(F32)
    rest = value - high
    mid = rest.astype(BF16).astype(F32)
    return high, mid, rest - mid


def outgoing_kernel(low_ref, gl_ref, ul_ref, og_ref, att_ref, lse_ref, out_ref):
    rank = gl_ref.shape[1]
    tokens, width = og_ref.shape
    heads = width // HD
    outer = (
        og_ref[...].astype(F32)
        + mm(low_ref[:, :rank], gl_ref[...], NT)
        + mm(low_ref[:, rank : 2 * rank], ul_ref[...], NT)
    ).astype(BF16)
    for place in range(out_ref.shape[0]):
        out_ref[place, :tokens, :] = outer
    product = outer.astype(F32) * att_ref[...].astype(F32)
    stats = []
    for kind in range(2):
        for half in range(2):
            mine = slice(half * HALF, (half + 1) * HALF)
            pieces = []
            for head in range(heads):
                if kind == 0:
                    column = lse_ref[head, mine, :]
                else:
                    column = jnp.sum(
                        product[mine, head * HD : (head + 1) * HD], axis=1, keepdims=True
                    )
                pieces.append(as_rows(column))
            stats.append(jnp.concatenate(pieces, axis=1))
    block = jnp.concatenate(stats, axis=0)
    parts = split3(block)
    block = jnp.concatenate(list(parts) + [jnp.zeros_like(block)], axis=0).astype(BF16)
    for place in range(out_ref.shape[0]):
        out_ref[place, tokens:, :] = block


def query_grad_kernel(
    order_ref, lens_ref, q_ref, att_ref, lse_ref, out_copies_ref, *refs
):
    blocks, (out_ref, inv_ref, kv_ref, do_ref, sems) = refs[:BLOCKS], refs[BLOCKS:]
    copies = fetch(blocks, kv_ref, sems)
    copies.append(
        pltpu.make_async_copy(
            out_copies_ref.at[0, pl.ds(0, do_ref.shape[0])], do_ref, sems.at[len(copies)]
        )
    )
    copies[-1].start()
    fill_slots(order_ref, inv_ref)
    edges = doc_edges(lens_ref)
    width = q_ref.shape[1]
    heads = width // HD
    settle(copies)
    for half in range(2):
        first, turns, rows, starts = query_range(order_ref, edges, half)
        mine = pl.ds(half * HALF, HALF)
        deltas, norms = [], []
        for head in range(heads):
            cols = slice(head * HD, (head + 1) * HD)
            deltas.append(
                jnp.sum(
                    do_ref[mine, cols].astype(F32) * att_ref[mine, cols].astype(F32),
                    axis=1,
                    keepdims=True,
                )
            )
            norms.append(lse_ref[head, mine, :1])

        def step(turn, carried):
            base = first + turn * CHUNK
            slots = slots_of(inv_ref, base)
            keys = rows_of(kv_ref, slots, slice(0, width))
            values = rows_of(kv_ref, slots, slice(width, 2 * width))
            ok = key_mask(base, rows, starts)
            out = []
            for head in range(heads):
                cols = slice(head * HD, (head + 1) * HD)
                raw = mm(q_ref[mine, cols], keys[:, cols], NT)
                weights = jnp.exp2(jnp.where(ok, raw * FACTOR2 - norms[head], LOW))
                back = mm(do_ref[mine, cols], values[:, cols], NT)
                grads = (weights * (back - deltas[head]) * FACTOR).astype(BF16)
                out.append(carried[head] + mm(grads, keys[:, cols], NN))
            return tuple(out)

        zero = jnp.zeros((HALF, HD), F32)
        sums = lax.fori_loop(0, turns, step, (zero,) * heads)
        for head in range(heads):
            out_ref[mine, head * HD : (head + 1) * HD] = sums[head].astype(BF16)


def key_grad_kernel(
    order_ref, lens_ref, k_ref, v_ref, mine_ref, other_ref, all_q_ref,
    gk_ref, gv_ref, inv_ref, stat_ref, q_ref, do_ref, sems
):
    copies = fetch_pair(mine_ref, other_ref, do_ref, sems, 0)
    copies.append(pltpu.make_async_copy(all_q_ref, q_ref, sems.at[2]))
    copies[-1].start()
    fill_slots(order_ref, inv_ref)
    edges = doc_edges(lens_ref)
    heads = k_ref.shape[1] // HD
    tokens = k_ref.shape[0]
    settle(copies)
    for owner in range(GROUP):
        stats = do_ref[owner // 2, owner % 2, tokens:, :].astype(F32)
        stat_ref[owner] = stats[0:4] + stats[4:8] + stats[8:12]
    for half in range(2):
        block = order_ref[2 * own_slot() + half]
        last = end_of(edges, block * HALF + HALF - 1)
        turns = ((last - 1) // HALF - block + CHUNK) // CHUNK
        rows = block * HALF + lax.broadcasted_iota(jnp.int32, (HALF, 1), 0)
        ends = end_of(edges, rows)
        mine = pl.ds(half * HALF, HALF)

        def step(turn, carried):
            base = block + turn * CHUNK
            slots = slots_of(inv_ref, base)
            queries = rows_of(q_ref, slots, slice(None))
            outers = rows_of(do_ref, slots, slice(None))
            norms, deltas = [], []
            for slot in slots:
                norms.append(stat_ref[slot // 2, pl.ds(slot % 2, 1), :])
                deltas.append(stat_ref[slot // 2, pl.ds(2 + slot % 2, 1), :])
            lanes = base * HALF + lax.broadcasted_iota(jnp.int32, (HALF, WIDE), 1)
            ok = (lanes >= rows) & (lanes < ends)
            out = []
            for head in range(heads):
                cols = slice(head * HD, (head + 1) * HD)
                norm = jnp.concatenate([item[:, cols] for item in norms], axis=1)
                delta = jnp.concatenate([item[:, cols] for item in deltas], axis=1)
                raw = mm(k_ref[mine, cols], queries[:, cols], NT)
                weights = jnp.exp2(jnp.where(ok, raw * FACTOR2 - norm, LOW))
                back = mm(v_ref[mine, cols], outers[:, cols], NT)
                grads = (weights * (back - delta) * FACTOR).astype(BF16)
                key_sum, value_sum = carried[head]
                out.append(
                    (
                        key_sum + mm(grads, queries[:, cols], NN),
                        value_sum + mm(weights.astype(BF16), outers[:, cols], NN),
                    )
                )
            return tuple(out)

        zero = jnp.zeros((HALF, HD), F32)
        sums = lax.fori_loop(0, turns, step, ((zero, zero),) * heads)
        for head in range(heads):
            cols = slice(head * HD, (head + 1) * HD)
            gk_ref[mine, cols] = sums[head][0].astype(BF16)
            gv_ref[mine, cols] = sums[head][1].astype(BF16)


def call(
    kernel, outs, scalars=(), arrays=(), remote=(), scratch=(), flops=0, moved=0, limit=VMEM_BYTES
):
    smem = pl.BlockSpec(memory_space=pltpu.SMEM)
    vmem = pl.BlockSpec(memory_space=pltpu.VMEM)
    anywhere = pl.BlockSpec(memory_space=pl.ANY)
    return pl.pallas_call(
        kernel,
        out_shape=tuple(jax.ShapeDtypeStruct(shape, kind) for shape, kind in outs),
        in_specs=[smem] * len(scalars) + [vmem] * len(arrays) + [anywhere] * len(remote),
        out_specs=tuple([vmem] * len(outs)),
        scratch_shapes=list(scratch),
        compiler_params=pltpu.CompilerParams(vmem_limit_bytes=limit),
        cost_estimate=pl.CostEstimate(flops=flops, bytes_accessed=moved, transcendentals=0),
    )(*scalars, *arrays, *remote)


def exchange(value, axis):
    return lax.all_to_all(value, axis, split_axis=0, concat_axis=0, tiled=True)


def head_sum(*held):
    rows, width = held[0].shape[0], sum(item.shape[1] for item in held)
    (copies,) = call(
        sum_kernel, (((rows, width), BF16),), arrays=held, moved=rows * width * 4
    )
    return copies


def token_total(terms):
    pieces, rows, width = terms.shape
    return call(
        token_sum_kernel,
        (((rows // 3, width), F32),) * 3,
        arrays=(exchange(terms, CTX),),
        moved=pieces * rows * width * 2,
    )


def send(value, up, across, other):
    def target(place):
        row, pair, core = place // 4, (place // 2) % 2, place % 2
        return ((row + up) % 4) * 4 + (pair + across) % 2 * 2 + (core + other) % 2

    return lax.ppermute(value, CTX, [(place, target(place)) for place in range(GROUP)])


def packed(blocks):
    rows, width = blocks[0].shape
    (pack,) = call(
        pack_kernel,
        (((PACKED * rows, width), BF16),),
        arrays=blocks,
        moved=4 * PACKED * rows * width,
    )
    return send(pack, 0, 0, 1)


def gather(own, part):
    held = exchange(part, "head")
    stage = (send(own, 1, 0, 0), send(own, 3, 0, 0), send(own, 0, 1, 0))
    own, below, above, beside = lax.optimization_barrier((own, *stage))
    first = (own, below, above, beside)
    stage = (
        send(below, 0, 1, 0), send(beside, 3, 0, 0), send(below, 1, 0, 0), send(below, 1, 1, 0)
    )
    *second, held = lax.optimization_barrier((*stage, held))
    return [*first, *second, packed(first), packed(second)], held


def after(value, *others):
    return lax.optimization_barrier((value, *others))[0]


def local(
    query,
    keys,
    values,
    out_grad,
    gate_left,
    up_left,
    gate_right,
    up_right,
    down_left,
    down_right,
    block_order,
    doc_lengths,
):
    tokens, width = query.shape
    heads = width // HD
    rank = gate_left.shape[1]
    units = down_left.shape[0]
    chips, cores = lax.axis_size("chip"), lax.axis_size("core")
    count = chips * cores
    everything = count * tokens
    places = (block_order, doc_lengths)
    inverse = pltpu.SMEM(block_order.shape, jnp.int32)
    gate_right_t, up_right_t = gate_right.T, up_right.T

    joined, part = call(
        first_kernel,
        (((tokens, 2 * width), BF16), ((tokens, rank), BF16)),
        arrays=(keys, values, out_grad, down_right),
        flops=2 * tokens * rank * width,
        moved=2 << 20,
        limit=60 * 1024 * 1024,
    )
    blocks, held = gather(joined, part)
    all_queries = lax.all_gather(after(query, blocks[6]), CTX, axis=0, tiled=True).reshape(
        chips, cores, tokens, width
    )

    attended, log_norm, part = call(
        forward_kernel,
        (
            ((tokens, width), BF16),
            ((heads, tokens, HALF), F32),
            ((tokens, 2 * rank), BF16),
        ),
        places,
        (query, gate_left, up_left),
        blocks,
        (
            inverse,
            pltpu.VMEM((CHUNKS, heads, HALF, WIDE), F32),
            pltpu.VMEM((chips, cores, tokens, 2 * width), BF16),
            pltpu.SemaphoreType.DMA((GROUP,)),
        ),
        flops=4 * tokens * everything * width,
        moved=64 << 20,
    )
    low = exchange(head_sum(exchange(part, "head"), held), "head")

    back_part, hidden, grad_gate, grad_up, mark = call(
        middle_kernel,
        (
            ((tokens, 3 * rank), BF16),
            ((tokens, units), BF16),
            ((tokens, units), BF16),
            ((tokens, units), BF16),
            ((16, HALF), BF16),
        ),
        arrays=(low, gate_right_t, up_right_t, down_left),
        scratch=(pltpu.VMEM((tokens, 3 * rank), F32),),
        flops=12 * tokens * rank * units,
        moved=4 << 20,
    )
    mark = lax.ppermute(mark, "core", [(0, 1), (1, 0)])
    copies = head_sum(exchange(back_part, "head"))
    back = exchange(copies, "head")

    (terms,) = call(
        right_terms_kernel,
        (((count, 3 * rank // count, units), BF16),),
        arrays=(low, grad_gate, grad_up, after(hidden, mark)),
        flops=6 * tokens * rank * units,
        moved=4 << 20,
    )
    held = lax.psum_scatter(
        terms.reshape(3 * rank, units), CTX, scatter_dimension=0, tiled=True
    )

    (outgoing,) = call(
        outgoing_kernel,
        (((chips, tokens + STATS, width), BF16),),
        arrays=(back, gate_left, up_left, out_grad, attended, log_norm),
        flops=4 * tokens * rank * width,
        moved=1 << 30,
    )
    mine = exchange(outgoing, "chip")
    (terms,) = call(
        left_terms_kernel,
        (((count, 3 * rank // count, width), BF16),),
        arrays=(back, attended, out_grad),
        flops=6 * tokens * rank * width,
        moved=2 << 20,
    )
    (grad_query,) = call(
        query_grad_kernel,
        (((tokens, width), BF16),),
        places,
        (query, attended, log_norm),
        (outgoing, *blocks),
        (
            inverse,
            pltpu.VMEM((chips, cores, tokens, 2 * width), BF16),
            pltpu.VMEM((tokens, width), BF16),
            pltpu.SemaphoreType.DMA((GROUP + 1,)),
        ),
        flops=6 * tokens * everything * width // 2,
        moved=6 << 20,
    )
    mine, grad_query, terms = lax.optimization_barrier((mine, grad_query, terms))
    other = lax.ppermute(mine, "core", [(0, 1), (1, 0)])
    left_sums = token_total(after(terms, other))
    grad_keys, grad_values = call(
        key_grad_kernel,
        (((tokens, width), BF16), ((tokens, width), BF16)),
        places,
        (keys, values),
        (mine, other, all_queries),
        (
            inverse,
            pltpu.VMEM((count, 4, width), F32),
            pltpu.VMEM((chips, cores, tokens, width), BF16),
            pltpu.VMEM((chips, cores, tokens + STATS, width), BF16),
            pltpu.SemaphoreType.DMA((3,)),
        ),
        flops=8 * tokens * everything * width // 2,
        moved=1 << 30,
    )
    right_sums = call(
        cast_kernel,
        (((rank // count, units), F32),) * 3,
        arrays=(after(held, grad_keys),),
        moved=1 << 19,
    )
    return (
        grad_query,
        grad_keys,
        grad_values,
        left_sums[0].T,
        left_sums[1].T,
        right_sums[2].T,
        right_sums[0],
        right_sums[1],
        left_sums[2],
    )


def solution(mesh):
    count = mesh.shape["ctx"]
    mesh = jax.sharding.Mesh(
        mesh.devices.reshape(count // 2, 2, mesh.shape["head"]), ("chip", "core", "head")
    )
    ctx = CTX
    in_specs = (
        P(ctx, "head"),
        P(ctx, "head"),
        P(ctx, "head"),
        P(ctx, "head"),
        P("head", None),
        P("head", None),
        P(None, "head"),
        P(None, "head"),
        P("head", None),
        P(None, "head"),
        P(),
        P(),
    )
    out_specs = (
        P(ctx, "head"),
        P(ctx, "head"),
        P(ctx, "head"),
        P("head", ctx),
        P("head", ctx),
        P("head", ctx),
        P(ctx, "head"),
        P(ctx, "head"),
        P(ctx, "head"),
    )
    return jax.shard_map(local, mesh=mesh, in_specs=in_specs, out_specs=out_specs, check_vma=False)
```

time: 702 us -> 232 us (0.33)
  waiting for transfers between devices: 396 us -> 66.8 us
  blocking collectives: 196 us -> 54.3 us
  matrix products: 50.5 us -> 0 us
  starting transfers between devices: 10.7 us -> 44.9 us
  Pallas kernels: 0 us -> 28.1 us
  other arithmetic: 20.1 us -> 0 us
  local copies, waits for them, and re-layouts: 11.8 us -> 21.7 us
    ppermute x64 -> x10, waiting for transfers between devices: 207 us -> 11.5 us  [the longest x9 8.79 us: send(): lax.ppermute(value, CTX, [(place, target(place)) for place in range(GROUP)])]
    psum x2 -> x0, blocking collectives: 196 us -> none  [rank_total(): summed = lax.psum(partials, 'head')]
    reduce_scatter x6 -> x1, waiting for transfers between devices: 120 us -> 13.2 us  [local(): lax.psum_scatter(terms.reshape(3 * rank, units), CTX, scatter_dimension=0...]
    all_gather x2 -> x1, waiting for transfers between devices: 68 us -> 0.02 us  [local(): lax.all_gather(after(query, blocks[6]), CTX, axis=0, tiled=True)]
    all_to_all x0 -> x2, blocking collectives: none -> 54.3 us  [exchange(): return lax.all_to_all(value, axis, split_axis=0, concat_axis=0, tiled=True)]
    dot_general x99 -> x0, matrix products: 50.5 us -> none  [the longest x17 8.33 us: tile_scores(): jnp.einsum('qhd,khd->hqk', query_heads, key_heads, preferred_element_type...]
    all_to_all x0 -> x5, waiting for transfers between devices: none -> 41.3 us  [exchange(): return lax.all_to_all(value, axis, split_axis=0, concat_axis=0, tiled=True)]
    all_to_all x0 -> x5, starting transfers between devices: none -> 36.1 us  [exchange(): return lax.all_to_all(value, axis, split_axis=0, concat_axis=0, tiled=True)]
  transfers between devices with their start and end apart: 72 -> 17, of which waited for: 36 -> 10; matrix products, arithmetic and copies ran while one was open for 8% -> 0% of each run, Pallas kernels for 0% -> 9%
where the time goes in v1:
time: 232 us; the launch traced here: 230 us
  waiting for transfers between devices  66.8 us (29%)
  blocking collectives  54.3 us (23%)
  starting transfers between devices  44.9 us (19%)
  Pallas kernels  28.1 us (12%)
  local copies, waits for them, and re-layouts  21.7 us (9%)
  between operations  14.4 us (6%)
    all_to_all x2, blocking collectives, exchange(): return lax.all_to_all(value, axis, split_axis=0, concat_axis=0, tiled=True)  54.3 us
    all_to_all x5, waiting for transfers between devices, exchange(): return lax.all_to_all(value, axis, split_axis=0, concat_axis=0, tiled=True)  41.3 us
    all_to_all x5, starting transfers between devices, exchange(): return lax.all_to_all(value, axis, split_axis=0, concat_axis=0, tiled=True)  36.1 us
    pallas_call x14, Pallas kernels, call(): pl.pallas_call(kernel, out_shape=tuple((jax.ShapeDtypeStruct(shape, kind)...  28.1 us
    unnamed x98, local copies, waits for them, and re-layouts  21.7 us
    reduce_scatter x1, waiting for transfers between devices, local(): lax.psum_scatter(terms.reshape(3 * rank, units), CTX, scatter_dimension=0...  13.2 us
    ppermute x9, waiting for transfers between devices, send(): lax.ppermute(value, CTX, [(place, target(place)) for place in range(GROUP)])  8.79 us
    ppermute x9, starting transfers between devices, send(): lax.ppermute(value, CTX, [(place, target(place)) for place in range(GROUP)])  8.56 us
  transfers between devices with their start and end apart: 17, of which 10 were waited for; matrix products, arithmetic and copies ran while one was open for 0% of the time, Pallas kernels for 9%

profile of v1, /device:TPU:4, one launch (start us, length us, event | category | flops | bytes accessed | tf_op | source)
XLA Modules:
  0.0 230.2 jit_solution(16322731278910701903)
XLA Ops:
  7.2 2.1 shard_map.187
  9.3 1.6 collective-permute-start
  10.9 1.7 collective-permute-start.1
  12.5 1.2 collective-permute-start.2
  13.7 11.4 %all-to-all-start = ((bf16[16,16,512]{2,1,0:T(8,128)(2,1)}), bf16[16,16,512]{2,1,0:T(8,128)(2,1)}, u32[]{:S(2)}, u32[]{:S(2)}) async-start(bf16[16,16,512]{2,1,0:T(8,128)(2,1)} %bitcast.29), calls=%async_computation | async-start | bytes 524288 | tf_op jit(solution)/shard_map/all_to_all | solution.py:485
  26.2 1.8 collective-permute-start.4
  30.1 1.1 shard_map.188
  31.3 4.0 %all-to-all-done = bf16[16,16,512]{2,1,0:T(8,128)(2,1)} async-done(((bf16[16,16,512]{2,1,0:T(8,128)(2,1)}), bf16[16,16,512]{2,1,0:T(8,128)(2,1)}, u32[]{:S(2)}, u32[]{:S(2)}) %all-to-all-start) | async-done | bytes 262176 | tf_op jit(solution)/shard_map/all_to_all | solution.py:485
  35.3 1.3 collective-permute-done.3.refs_0_.refs_4_
  37.2 4.3 %collective-permute-done.6.refs_3_.refs_7_ = bf16[256,512]{1,0:T(8,128)(2,1)S(1)} collective-permute-done((bf16[256,512]{1,0:T(8,128)(2,1)S(1)}, bf16[256,512]{1,0:T(8,128)(2,1)S(1)}, u32[]{:S(2)}, u32[]{:S(2)}) %collective-permute-start.6) | collective-permute-done | bytes 262176 | tf_op jit(solution)/shard_map/ppermute | solution.py:511
  41.6 2.6 %collective-permute-done.8.refs_9_ = bf16[1024,512]{1,0:T(8,128)(2,1)S(1)} collective-permute-done((bf16[1024,512]{1,0:T(8,128)(2,1)S(1)}, bf16[1024,512]{1,0:T(8,128)(2,1)S(1)}, u32[]{:S(2)}, u32[]{:S(2)}) %collective-permute-start.8) | collective-permute-done | bytes 1048608 | tf_op jit(solution)/shard_map/ppermute | solution.py:511
  46.2 4.1 %shard_map.190 = (bf16[256,256]{1,0:T(8,128)(2,1)S(1)}, f32[2,256,128]{2,1,0:T(8,128)S(1)}, bf16[256,1024]{1,0:T(8,128)(2,1)S(1)}) custom-call(s32[32]{0:T(128)S(1)} %copy-done.44, s32[4]{0:T(128)S(1)} %copy-done.45, bf16[256,256]{1,0:T(8,128)(2,1)S(1)} %copy-done.23, bf16[256,512]{1,0:T(8,128)(2,1)S(1)} %copy-done.30, bf16[256,512]{1,0:T(8,128)(2,1)S(1)} %copy-done.32, ...), custom_call_target="tpu_custom_call" | custom-call | flops 1073741824 | bytes 67108864 | tf_op jit(solution)/shard_map/pallas_call | solution.py:473
  51.9 9.6 %all-to-all-start.1 = ((bf16[16,16,1024]{2,1,0:T(8,128)(2,1)}), bf16[16,16,1024]{2,1,0:T(8,128)(2,1)S(1)}, u32[]{:S(2)}, u32[]{:S(2)}) async-start(bf16[16,16,1024]{2,1,0:T(8,128)(2,1)} %bitcast.26), calls=%async_computation.1 | async-start | bytes 1048576 | tf_op jit(solution)/shard_map/all_to_all | solution.py:485
  62.2 16.7 %all-to-all-done.1 = bf16[16,16,1024]{2,1,0:T(8,128)(2,1)S(1)} async-done(((bf16[16,16,1024]{2,1,0:T(8,128)(2,1)}), bf16[16,16,1024]{2,1,0:T(8,128)(2,1)S(1)}, u32[]{:S(2)}, u32[]{:S(2)}) %all-to-all-start.1) | async-done | bytes 524320 | tf_op jit(solution)/shard_map/all_to_all | solution.py:485
  78.9 1.1 shard_map.191
  80.1 27.4 %all_to_all.66 = bf16[16,16,1536]{2,1,0:T(8,128)(2,1)S(1)} all-to-all(bf16[16,16,1536]{2,1,0:T(8,128)(2,1)S(1)} %bitcast.19), channel_id=1, replica_groups=mesh['chip'=8,'core'=2,'head'=16] {'head'}, dimensions={0} | all-to-all | bytes 1572864 | tf_op jit(solution)/shard_map/all_to_all | solution.py:485
  107.4 2.2 shard_map.192
  109.7 26.9 %all_to_all.67 = bf16[16,16,1536]{2,1,0:T(8,128)(2,1)S(1)} all-to-all(bf16[16,16,1536]{2,1,0:T(8,128)(2,1)S(1)} %bitcast.25), channel_id=1, replica_groups=mesh['chip'=8,'core'=2,'head'=16] {'head'}, dimensions={0} | all-to-all | bytes 1572864 | tf_op jit(solution)/shard_map/all_to_all | solution.py:485
  136.6 1.0 shard_map.193
  137.6 6.4 %all-to-all-start.4 = ((bf16[16,16,1536]{2,1,0:T(8,128)(2,1)}), bf16[16,16,1536]{2,1,0:T(8,128)(2,1)S(1)}, u32[]{:S(2)}, u32[]{:S(2)}) async-start(bf16[16,16,1536]{2,1,0:T(8,128)(2,1)} %bitcast.10), calls=%async_computation.4 | async-start | bytes 1572864 | tf_op jit(solution)/shard_map/all_to_all | solution.py:485
  147.2 2.2 shard_map.199
  149.4 13.6 %all-to-all-done.4 = bf16[16,16,1536]{2,1,0:T(8,128)(2,1)S(1)} async-done(((bf16[16,16,1536]{2,1,0:T(8,128)(2,1)}), bf16[16,16,1536]{2,1,0:T(8,128)(2,1)S(1)}, u32[]{:S(2)}, u32[]{:S(2)}) %all-to-all-start.4) | async-done | bytes 786464 | tf_op jit(solution)/shard_map/all_to_all | solution.py:485
  164.0 1.5 shard_map.194.out_copies_ref
  165.5 3.7 %all-to-all-start.5 = ((bf16[8,272,256]{2,1,0:T(8,128)(2,1)}), bf16[8,272,256]{2,1,0:T(8,128)(2,1)S(1)}, u32[]{:S(2)}, u32[]{:S(2)}) async-start(bf16[8,272,256]{2,1,0:T(8,128)(2,1)} %shard_map.194.out_copies_ref), calls=%async_computation.5 | async-start | bytes 2228224 | tf_op jit(solution)/shard_map/all_to_all | solution.py:485
  178.3 5.5 %shard_map.195 = bf16[256,256]{1,0:T(8,128)(2,1)} custom-call(s32[32]{0:T(128)S(1)} %copy-done.44, s32[4]{0:T(128)S(1)} %copy-done.45, bf16[256,256]{1,0:T(8,128)(2,1)S(1)} %copy-done.24, bf16[256,256]{1,0:T(8,128)(2,1)S(1)} %copy-done.22, f32[2,256,128]{2,1,0:T(8,128)S(1)} %copy-done.29, bf16[8,272,256]{2,1,0:T(8,128)(2,1)} %shard_map.194.out_copies_ref, ...), custom_call_target="tpu_custom_call" | custom-call | flops 805306368 | bytes 6291456 | tf_op jit(solution)/shard_map/pallas_call | solution.py:473
  183.8 7.0 %all-to-all-done.5.mine_ref = bf16[8,272,256]{2,1,0:T(8,128)(2,1)S(1)} async-done(((bf16[8,272,256]{2,1,0:T(8,128)(2,1)}), bf16[8,272,256]{2,1,0:T(8,128)(2,1)S(1)}, u32[]{:S(2)}, u32[]{:S(2)}) %all-to-all-start.5) | async-done | bytes 1114144 | tf_op jit(solution)/shard_map/all_to_all | solution.py:485
  190.8 2.8 %collective-permute-done.9.other_ref = bf16[8,272,256]{2,1,0:T(8,128)(2,1)S(1)} collective-permute-done((bf16[8,272,256]{2,1,0:T(8,128)(2,1)S(1)}, bf16[8,272,256]{2,1,0:T(8,128)(2,1)S(1)}, u32[]{:S(2)}, u32[]{:S(2)}) %collective-permute-start.9) | collective-permute-done | bytes 1114144 | tf_op jit(solution)/shard_map/ppermute | solution.py:660
  194.6 4.9 %all-to-all-start.6 = ((bf16[16,96,256]{2,1,0:T(8,128)(2,1)}), bf16[16,96,256]{2,1,0:T(8,128)(2,1)S(1)}, u32[]{:S(2)}, u32[]{:S(2)}) async-start(bf16[16,96,256]{2,1,0:T(8,128)(2,1)} %copy-done.2), calls=%async_computation.6 | async-start | bytes 1572864 | tf_op jit(solution)/shard_map/all_to_all | solution.py:485
  199.6 1.6 copy-done.17
  201.2 1.2 copy-done.26
  202.4 5.4 %shard_map.197 = (bf16[256,256]{1,0:T(8,128)(2,1)}, bf16[256,256]{1,0:T(8,128)(2,1)}) custom-call(s32[32]{0:T(128)S(1)} %copy-done.44, s32[4]{0:T(128)S(1)} %copy-done.45, bf16[256,256]{1,0:T(8,128)(2,1)S(1)} %copy-done.34, bf16[256,256]{1,0:T(8,128)(2,1)S(1)} %copy-done.35, bf16[8,272,256]{2,1,0:T(8,128)(2,1)S(1)} %all-to-all-done.5.mine_ref, ...), custom_call_target="tpu_custom_call" | custom-call | flops 1073741824 | bytes 1073741824 | tf_op jit(solution)/shard_map/pallas_call | solution.py:473
  207.8 13.2 %reduce-scatter.2.cloned.1.call-done.held_ref = bf16[96,688]{1,0:T(8,128)(2,1)} async-done(((bf16[1536,688]{1,0:T(8,128)(2,1)}), bf16[96,688]{1,0:T(8,128)(2,1)}) %reduce-scatter.2.cloned.1.call-update) | async-done | bytes 132112 | tf_op jit(solution)/shard_map/reduce_scatter | solution.py:625
  (118 shorter events, 24.7 us)
Async XLA Ops:
  9.3 15.9 %collective-permute-start = (bf16[256,512]{1,0:T(8,128)(2,1)}, bf16[256,512]{1,0:T(8,128)(2,1)S(1)}, u32[]{:S(2)}, u32[]{:S(2)}) collective-permute-start(bf16[256,512]{1,0:T(8,128)(2,1)} %get-tuple-element.42.refs_0_), channel_id=1, source_target_pairs={{0,64},{16,80},{32,96},{48,112},{64,128},{80,144},{96,160},{112,17... | collective-permute-start | bytes 786440 | tf_op jit(solution)/shard_map/ppermute | solution.py:511
  10.9 14.3 %collective-permute-start.1 = (bf16[256,512]{1,0:T(8,128)(2,1)}, bf16[256,512]{1,0:T(8,128)(2,1)S(1)}, u32[]{:S(2)}, u32[]{:S(2)}) collective-permute-start(bf16[256,512]{1,0:T(8,128)(2,1)} %get-tuple-element.42.refs_0_), channel_id=1, source_target_pairs={{0,192},{16,208},{32,224},{48,240},{64,0},{80,16},{96,32},{112,48}... | collective-permute-start | bytes 786440 | tf_op jit(solution)/shard_map/ppermute | solution.py:511
  12.5 12.7 %collective-permute-start.2 = (bf16[256,512]{1,0:T(8,128)(2,1)}, bf16[256,512]{1,0:T(8,128)(2,1)S(1)}, u32[]{:S(2)}, u32[]{:S(2)}) collective-permute-start(bf16[256,512]{1,0:T(8,128)(2,1)} %get-tuple-element.42.refs_0_), channel_id=1, source_target_pairs={{0,32},{16,48},{32,0},{48,16},{64,96},{80,112},{96,64},{112,80},{1... | collective-permute-start | bytes 786440 | tf_op jit(solution)/shard_map/ppermute | solution.py:511
  13.7 21.6 %all-to-all-start = ((bf16[16,16,512]{2,1,0:T(8,128)(2,1)}), bf16[16,16,512]{2,1,0:T(8,128)(2,1)}, u32[]{:S(2)}, u32[]{:S(2)}) async-start(bf16[16,16,512]{2,1,0:T(8,128)(2,1)} %bitcast.29), calls=%async_computation | async-start | bytes 524288 | tf_op jit(solution)/shard_map/all_to_all | solution.py:485
  25.2 19.1 %copy-start.5 = (bf16[256,512]{1,0:T(8,128)(2,1)}, bf16[256,512]{1,0:T(8,128)(2,1)S(1)}, u32[]{:S(2)}) copy-start(bf16[256,512]{1,0:T(8,128)(2,1)S(1)} %collective-permute-done.1.refs_2_) | copy-start | bytes 786436
  25.2 19.1 %copy-start.7 = (bf16[256,512]{1,0:T(8,128)(2,1)}, bf16[256,512]{1,0:T(8,128)(2,1)S(1)}, u32[]{:S(2)}) copy-start(bf16[256,512]{1,0:T(8,128)(2,1)S(1)} %collective-permute-done.2.refs_3_) | copy-start | bytes 786436
  25.2 11.4 %collective-permute-start.3 = (bf16[256,512]{1,0:T(8,128)(2,1)S(1)}, bf16[256,512]{1,0:T(8,128)(2,1)S(1)}, u32[]{:S(2)}, u32[]{:S(2)}) collective-permute-start(bf16[256,512]{1,0:T(8,128)(2,1)S(1)} %collective-permute-done.refs_1_), channel_id=1, source_target_pairs={{0,32},{16,48},{32,0},{48,16},{64,96},{80,112},{96,64},{112,80},{1... | collective-permute-start | bytes 786440 | tf_op jit(solution)/shard_map/ppermute | solution.py:511
  26.2 10.4 %collective-permute-start.4 = (bf16[256,512]{1,0:T(8,128)(2,1)S(1)}, bf16[256,512]{1,0:T(8,128)(2,1)S(1)}, u32[]{:S(2)}, u32[]{:S(2)}) collective-permute-start(bf16[256,512]{1,0:T(8,128)(2,1)S(1)} %collective-permute-done.2.refs_3_), channel_id=1, source_target_pairs={{0,192},{16,208},{32,224},{48,240},{64,0},{80,16},{96,32},{112,48}... | collective-permute-start | bytes 786440 | tf_op jit(solution)/shard_map/ppermute | solution.py:511
  28.0 9.2 %collective-permute-start.5 = (bf16[256,512]{1,0:T(8,128)(2,1)S(1)}, bf16[256,512]{1,0:T(8,128)(2,1)S(1)}, u32[]{:S(2)}, u32[]{:S(2)}) collective-permute-start(bf16[256,512]{1,0:T(8,128)(2,1)S(1)} %collective-permute-done.refs_1_), channel_id=1, source_target_pairs={{0,64},{16,80},{32,96},{48,112},{64,128},{80,144},{96,160},{112,17... | collective-permute-start | bytes 786440 | tf_op jit(solution)/shard_map/ppermute | solution.py:511
  28.2 13.3 %collective-permute-start.6 = (bf16[256,512]{1,0:T(8,128)(2,1)S(1)}, bf16[256,512]{1,0:T(8,128)(2,1)S(1)}, u32[]{:S(2)}, u32[]{:S(2)}) collective-permute-start(bf16[256,512]{1,0:T(8,128)(2,1)S(1)} %collective-permute-done.refs_1_), channel_id=1, source_target_pairs={{0,96},{16,112},{32,64},{48,80},{64,160},{80,176},{96,128},{112,14... | collective-permute-start | bytes 786440 | tf_op jit(solution)/shard_map/ppermute | solution.py:511
  31.2 10.4 %collective-permute-start.7 = (bf16[1024,512]{1,0:T(8,128)(2,1)}, bf16[1024,512]{1,0:T(8,128)(2,1)S(1)}, u32[]{:S(2)}, u32[]{:S(2)}) collective-permute-start(bf16[1024,512]{1,0:T(8,128)(2,1)} %shard_map.188), channel_id=1, source_target_pairs={{0,16},{16,0},{32,48},{48,32},{64,80},{80,64},{96,112},{112,96},{1... | collective-permute-start | bytes 3145736 | tf_op jit(solution)/shard_map/ppermute | solution.py:511
  36.6 13.7 %copy-start.9 = (bf16[256,512]{1,0:T(8,128)(2,1)}, bf16[256,512]{1,0:T(8,128)(2,1)S(1)}, u32[]{:S(2)}) copy-start(bf16[256,512]{1,0:T(8,128)(2,1)S(1)} %collective-permute-done.3.refs_0_.refs_4_) | copy-start | bytes 786436
  36.6 13.7 %copy-start.11 = (bf16[256,512]{1,0:T(8,128)(2,1)}, bf16[256,512]{1,0:T(8,128)(2,1)S(1)}, u32[]{:S(2)}) copy-start(bf16[256,512]{1,0:T(8,128)(2,1)S(1)} %collective-permute-done.4.refs_1_.refs_5_) | copy-start | bytes 786436
  41.5 2.7 %collective-permute-start.8 = (bf16[1024,512]{1,0:T(8,128)(2,1)S(1)}, bf16[1024,512]{1,0:T(8,128)(2,1)S(1)}, u32[]{:S(2)}, u32[]{:S(2)}) collective-permute-start(bf16[1024,512]{1,0:T(8,128)(2,1)S(1)} %shard_map.189), channel_id=1, source_target_pairs={{0,16},{16,0},{32,48},{48,32},{64,80},{80,64},{96,112},{112,96},{1... | collective-permute-start | bytes 3145736 | tf_op jit(solution)/shard_map/ppermute | solution.py:511
  51.1 112.0 %copy-start.20 = (bf16[256,256]{1,0:T(8,128)(2,1)}, bf16[256,256]{1,0:T(8,128)(2,1)S(1)}, u32[]{:S(2)}) copy-start(bf16[256,256]{1,0:T(8,128)(2,1)S(1)} %get-tuple-element.54.att_ref) | copy-start | bytes 393220
  51.9 27.0 %all-to-all-start.1 = ((bf16[16,16,1024]{2,1,0:T(8,128)(2,1)}), bf16[16,16,1024]{2,1,0:T(8,128)(2,1)S(1)}, u32[]{:S(2)}, u32[]{:S(2)}) async-start(bf16[16,16,1024]{2,1,0:T(8,128)(2,1)} %bitcast.26), calls=%async_computation.1 | async-start | bytes 1048576 | tf_op jit(solution)/shard_map/all_to_all | solution.py:485
  61.5 138.1 %all-gather.2.cloned.1.call-start = ((), (), s32[]{:S(2)}) async-start(), calls=%async_computation.8 | async-start | bytes 2228224 | tf_op jit(solution)/shard_map/all_gather | solution.py:575
  78.9 28.5 %copy-start.48 = (bf16[688,512]{1,0:T(8,128)(2,1)S(1)}, bf16[688,512]{1,0:T(8,128)(2,1)}, u32[]{:S(2)}) copy-start(bf16[688,512]{1,0:T(8,128)(2,1)} %dl_ref.1) | copy-start | bytes 2113540
  80.0 27.4 %copy-start.46 = (bf16[512,688]{0,1:T(8,128)(2,1)S(1)}, bf16[512,688]{0,1:T(8,128)(2,1)}, u32[]{:S(2)}) copy-start(bf16[512,688]{0,1:T(8,128)(2,1)} %param.18) | copy-start | bytes 2113540
  80.1 27.4 %copy-start.47 = (bf16[512,688]{0,1:T(8,128)(2,1)S(1)}, bf16[512,688]{0,1:T(8,128)(2,1)}, u32[]{:S(2)}) copy-start(bf16[512,688]{0,1:T(8,128)(2,1)} %param.19) | copy-start | bytes 2113540
  109.7 28.0 %copy-start.37 = (bf16[256,688]{1,0:T(8,128)(2,1)}, bf16[256,688]{1,0:T(8,128)(2,1)S(1)}, u32[]{:S(2)}) copy-start(bf16[256,688]{1,0:T(8,128)(2,1)S(1)} %get-tuple-element.67.hidden_ref) | copy-start | bytes 1056772
  109.7 28.0 %copy-start.39 = (bf16[256,688]{1,0:T(8,128)(2,1)}, bf16[256,688]{1,0:T(8,128)(2,1)S(1)}, u32[]{:S(2)}) copy-start(bf16[256,688]{1,0:T(8,128)(2,1)S(1)} %get-tuple-element.65.gg_ref) | copy-start | bytes 1056772
  109.7 28.0 %copy-start.41 = (bf16[256,688]{1,0:T(8,128)(2,1)}, bf16[256,688]{1,0:T(8,128)(2,1)S(1)}, u32[]{:S(2)}) copy-start(bf16[256,688]{1,0:T(8,128)(2,1)S(1)} %get-tuple-element.66.gu_ref) | copy-start | bytes 1056772
  137.6 25.4 %all-to-all-start.4 = ((bf16[16,16,1536]{2,1,0:T(8,128)(2,1)}), bf16[16,16,1536]{2,1,0:T(8,128)(2,1)S(1)}, u32[]{:S(2)}, u32[]{:S(2)}) async-start(bf16[16,16,1536]{2,1,0:T(8,128)(2,1)} %bitcast.10), calls=%async_computation.4 | async-start | bytes 1572864 | tf_op jit(solution)/shard_map/all_to_all | solution.py:485
  144.0 77.0 %reduce-scatter.2.cloned.1.call-start = ((), (), s32[]{:S(2)}) async-start(), calls=%async_computation.9 | async-start | bytes 2506752 | tf_op jit(solution)/shard_map/reduce_scatter | solution.py:625
  149.4 13.6 %copy-start.28 = (f32[2,256,128]{2,1,0:T(8,128)S(1)}, f32[2,256,128]{2,1,0:T(8,128)}, u32[]{:S(2)}) copy-start(f32[2,256,128]{2,1,0:T(8,128)} %copy-done.27) | copy-start | bytes 786436
  149.4 13.6 %copy-start.31 = (bf16[256,512]{1,0:T(8,128)(2,1)S(1)}, bf16[256,512]{1,0:T(8,128)(2,1)}, u32[]{:S(2)}) copy-start(bf16[256,512]{1,0:T(8,128)(2,1)} %gl_ref.3) | copy-start | bytes 786436
  165.5 25.3 %all-to-all-start.5 = ((bf16[8,272,256]{2,1,0:T(8,128)(2,1)}), bf16[8,272,256]{2,1,0:T(8,128)(2,1)S(1)}, u32[]{:S(2)}, u32[]{:S(2)}) async-start(bf16[8,272,256]{2,1,0:T(8,128)(2,1)} %shard_map.194.out_copies_ref), calls=%async_computation.5 | async-start | bytes 2228224 | tf_op jit(solution)/shard_map/all_to_all | solution.py:485
  183.8 15.8 %copy-start.34 = (bf16[256,256]{1,0:T(8,128)(2,1)S(1)}, bf16[256,256]{1,0:T(8,128)(2,1)}, u32[]{:S(2)}) copy-start(bf16[256,256]{1,0:T(8,128)(2,1)} %k_ref.3) | copy-start | bytes 393220
  183.8 15.8 %copy-start.35 = (bf16[256,256]{1,0:T(8,128)(2,1)S(1)}, bf16[256,256]{1,0:T(8,128)(2,1)}, u32[]{:S(2)}) copy-start(bf16[256,256]{1,0:T(8,128)(2,1)} %v_ref.3) | copy-start | bytes 393220
  190.8 2.8 %collective-permute-start.9 = (bf16[8,272,256]{2,1,0:T(8,128)(2,1)S(1)}, bf16[8,272,256]{2,1,0:T(8,128)(2,1)S(1)}, u32[]{:S(2)}, u32[]{:S(2)}) collective-permute-start(bf16[8,272,256]{2,1,0:T(8,128)(2,1)S(1)} %all-to-all-done.5.mine_ref), channel_id=1, source_target_pairs={{0,16},{16,0},{1,17},{17,1},{2,18},{18,2},{3,19},{19,3},{4,20},{20... | collective-permute-start | bytes 3342344 | tf_op jit(solution)/shard_map/ppermute | solution.py:660
  194.6 28.1 %all-to-all-start.6 = ((bf16[16,96,256]{2,1,0:T(8,128)(2,1)}), bf16[16,96,256]{2,1,0:T(8,128)(2,1)S(1)}, u32[]{:S(2)}, u32[]{:S(2)}) async-start(bf16[16,96,256]{2,1,0:T(8,128)(2,1)} %copy-done.2), calls=%async_computation.6 | async-start | bytes 1572864 | tf_op jit(solution)/shard_map/all_to_all | solution.py:485
  (34 other events, 119.5 us)
Sparse Core Ops, SparseCore 0:
  64.2 37.5 all-gather.1
  149.6 71.4 reduce-scatter.1

commit v2 on v1

--- a/solution.py
+++ b/solution.py
@@ -241,7 +241,7 @@
 
 
 def middle_kernel(
-    low_ref, grt_ref, urt_ref, dl_ref, back_ref, hidden_ref, gg_ref, gu_ref, mark_ref, acc_ref
+    low_ref, grt_ref, urt_ref, dl_ref, back_ref, out_ref, hidden_ref, gg_ref, gu_ref, acc_ref
 ):
     rank = dl_ref.shape[1]
     units = dl_ref.shape[0]
@@ -269,9 +269,14 @@
                 term = term + acc_ref[:, there]
             if base + 256 >= units:
                 back_ref[:, there] = term.astype(BF16)
-                mark_ref[...] = term[: mark_ref.shape[0], : mark_ref.shape[1]].astype(BF16)
             else:
                 acc_ref[:, there] = term
+    pairs = (
+        (low_ref.at[:, :rank], gg_ref),
+        (low_ref.at[:, rank : 2 * rank], gu_ref),
+        (low_ref.at[:, 2 * rank :], hidden_ref),
+    )
+    outer_terms(pairs, out_ref)
 
 
 def outer_terms(pairs, out_ref):
@@ -285,16 +290,6 @@
                 out_ref[base + piece, number * rows : (number + 1) * rows, :] = term[
                     piece * rows : (piece + 1) * rows
                 ]
-
-
-def right_terms_kernel(low_ref, gg_ref, gu_ref, hidden_ref, out_ref):
-    rank = low_ref.shape[1] // 3
-    pairs = (
-        (low_ref.at[:, :rank], gg_ref),
-        (low_ref.at[:, rank : 2 * rank], gu_ref),
-        (low_ref.at[:, 2 * rank :], hidden_ref),
-    )
-    outer_terms(pairs, out_ref)
 
 
 def left_terms_kernel(back_ref, att_ref, og_ref, out_ref):
@@ -597,34 +592,27 @@
     )
     low = exchange(head_sum(exchange(part, "head"), held), "head")
 
-    back_part, hidden, grad_gate, grad_up, mark = call(
+    back_part, terms = call(
         middle_kernel,
         (
             ((tokens, 3 * rank), BF16),
-            ((tokens, units), BF16),
-            ((tokens, units), BF16),
-            ((tokens, units), BF16),
-            ((16, HALF), BF16),
+            ((count, 3 * rank // count, units), BF16),
         ),
         arrays=(low, gate_right_t, up_right_t, down_left),
-        scratch=(pltpu.VMEM((tokens, 3 * rank), F32),),
-        flops=12 * tokens * rank * units,
+        scratch=(
+            pltpu.VMEM((tokens, units), BF16),
+            pltpu.VMEM((tokens, units), BF16),
+            pltpu.VMEM((tokens, units), BF16),
+            pltpu.VMEM((tokens, 3 * rank), F32),
+        ),
+        flops=18 * tokens * rank * units,
         moved=4 << 20,
     )
-    mark = lax.ppermute(mark, "core", [(0, 1), (1, 0)])
+    held = lax.psum_scatter(
+        terms.reshape(3 * rank, units), CTX, scatter_dimension=0, tiled=True
+    )
     copies = head_sum(exchange(back_part, "head"))
     back = exchange(copies, "head")
-
-    (terms,) = call(
-        right_terms_kernel,
-        (((count, 3 * rank // count, units), BF16),),
-        arrays=(low, grad_gate, grad_up, after(hidden, mark)),
-        flops=6 * tokens * rank * units,
-        moved=4 << 20,
-    )
-    held = lax.psum_scatter(
-        terms.reshape(3 * rank, units), CTX, scatter_dimension=0, tiled=True
-    )
 
     (outgoing,) = call(
         outgoing_kernel,

time: 232 us -> 232 us (level)
  Pallas kernels: 28.1 us -> 24.3 us
  waiting for transfers between devices: 66.8 us -> 70.3 us
    pallas_call x14 -> x13, Pallas kernels: 28.1 us -> 24.3 us  [call(): pl.pallas_call(kernel, out_shape=tuple((jax.ShapeDtypeStruct(shape, kind)...]
    all_to_all x5, waiting for transfers between devices: 41.3 us -> 44.6 us  [exchange(): return lax.all_to_all(value, axis, split_axis=0, concat_axis=0, tiled=True)]
    unnamed x98 -> x88, local copies, waits for them, and re-layouts: 21.7 us -> 20.2 us
  transfers between devices with their start and end apart: 17 -> 17, of which waited for: 10 -> 9; matrix products, arithmetic and copies ran while one was open for 0% -> 0% of each run, Pallas kernels for 9% -> 8%
where the time goes in v2:
time: 232 us; the launch traced here: 231 us
  waiting for transfers between devices  70.3 us (30%)
  blocking collectives  54.3 us (23%)
  starting transfers between devices  47.2 us (20%)
  Pallas kernels  24.3 us (10%)
  local copies, waits for them, and re-layouts  20.2 us (9%)
  between operations  14.4 us (6%)
    all_to_all x2, blocking collectives, exchange(): return lax.all_to_all(value, axis, split_axis=0, concat_axis=0, tiled=True)  54.3 us
    all_to_all x5, waiting for transfers between devices, exchange(): return lax.all_to_all(value, axis, split_axis=0, concat_axis=0, tiled=True)  44.6 us
    all_to_all x5, starting transfers between devices, exchange(): return lax.all_to_all(value, axis, split_axis=0, concat_axis=0, tiled=True)  37.3 us
    pallas_call x13, Pallas kernels, call(): pl.pallas_call(kernel, out_shape=tuple((jax.ShapeDtypeStruct(shape, kind)...  24.3 us
    unnamed x88, local copies, waits for them, and re-layouts  20.2 us
    reduce_scatter x1, waiting for transfers between devices, local(): lax.psum_scatter(terms.reshape(3 * rank, units), CTX, scatter_dimension=0...  12.8 us
    ppermute x9, starting transfers between devices, send(): lax.ppermute(value, CTX, [(place, target(place)) for place in range(GROUP)])  9.77 us
    ppermute x9, waiting for transfers between devices, send(): lax.ppermute(value, CTX, [(place, target(place)) for place in range(GROUP)])  8.8 us
  transfers between devices with their start and end apart: 17, of which 9 were waited for; matrix products, arithmetic and copies ran while one was open for 0% of the time, Pallas kernels for 8%

profile of v2, /device:TPU:4, one launch (start us, length us, event | category | flops | bytes accessed | tf_op | source)
XLA Modules:
  0.0 230.7 jit_solution(17985947317406172613)
XLA Ops:
  7.2 2.2 shard_map.187
  9.3 1.6 collective-permute-start
  10.9 1.7 collective-permute-start.1
  12.6 1.2 collective-permute-start.2
  13.8 11.4 %all-to-all-start = ((bf16[16,16,512]{2,1,0:T(8,128)(2,1)}), bf16[16,16,512]{2,1,0:T(8,128)(2,1)}, u32[]{:S(2)}, u32[]{:S(2)}) async-start(bf16[16,16,512]{2,1,0:T(8,128)(2,1)} %bitcast.29), calls=%async_computation | async-start | bytes 524288 | tf_op jit(solution)/shard_map/all_to_all | solution.py:480
  26.5 2.2 collective-permute-start.6
  28.8 1.7 collective-permute-start.4
  31.4 1.1 shard_map.188
  32.6 2.8 %all-to-all-done = bf16[16,16,512]{2,1,0:T(8,128)(2,1)} async-done(((bf16[16,16,512]{2,1,0:T(8,128)(2,1)}), bf16[16,16,512]{2,1,0:T(8,128)(2,1)}, u32[]{:S(2)}, u32[]{:S(2)}) %all-to-all-start) | async-done | bytes 262176 | tf_op jit(solution)/shard_map/all_to_all | solution.py:480
  35.3 1.3 collective-permute-done.3.refs_0_.refs_4_
  36.6 4.9 %collective-permute-done.6.refs_3_.refs_7_ = bf16[256,512]{1,0:T(8,128)(2,1)S(1)} collective-permute-done((bf16[256,512]{1,0:T(8,128)(2,1)S(1)}, bf16[256,512]{1,0:T(8,128)(2,1)S(1)}, u32[]{:S(2)}, u32[]{:S(2)}) %collective-permute-start.6) | collective-permute-done | bytes 262176 | tf_op jit(solution)/shard_map/ppermute | solution.py:506
  41.7 2.6 %collective-permute-done.8.refs_9_ = bf16[1024,512]{1,0:T(8,128)(2,1)S(1)} collective-permute-done((bf16[1024,512]{1,0:T(8,128)(2,1)S(1)}, bf16[1024,512]{1,0:T(8,128)(2,1)S(1)}, u32[]{:S(2)}, u32[]{:S(2)}) %collective-permute-start.8) | collective-permute-done | bytes 1048608 | tf_op jit(solution)/shard_map/ppermute | solution.py:506
  46.3 3.5 %shard_map.190 = (bf16[256,256]{1,0:T(8,128)(2,1)S(1)}, f32[2,256,128]{2,1,0:T(8,128)S(1)}, bf16[256,1024]{1,0:T(8,128)(2,1)S(1)}) custom-call(s32[32]{0:T(128)S(1)} %copy-done.39, s32[4]{0:T(128)S(1)} %copy-done.40, bf16[256,256]{1,0:T(8,128)(2,1)S(1)} %copy-done.24, bf16[256,512]{1,0:T(8,128)(2,1)S(1)} %copy-done.31, bf16[256,512]{1,0:T(8,128)(2,1)S(1)} %copy-done.33, ...), custom_call_target="tpu_custom_call" | custom-call | flops 1073741824 | bytes 67108864 | tf_op jit(solution)/shard_map/pallas_call | solution.py:468
  51.3 9.6 %all-to-all-start.1 = ((bf16[16,16,1024]{2,1,0:T(8,128)(2,1)}), bf16[16,16,1024]{2,1,0:T(8,128)(2,1)S(1)}, u32[]{:S(2)}, u32[]{:S(2)}) async-start(bf16[16,16,1024]{2,1,0:T(8,128)(2,1)} %bitcast.26), calls=%async_computation.1 | async-start | bytes 1048576 | tf_op jit(solution)/shard_map/all_to_all | solution.py:480
  61.7 16.7 %all-to-all-done.1 = bf16[16,16,1024]{2,1,0:T(8,128)(2,1)S(1)} async-done(((bf16[16,16,1024]{2,1,0:T(8,128)(2,1)}), bf16[16,16,1024]{2,1,0:T(8,128)(2,1)S(1)}, u32[]{:S(2)}, u32[]{:S(2)}) %all-to-all-start.1) | async-done | bytes 524320 | tf_op jit(solution)/shard_map/all_to_all | solution.py:480
  78.4 1.1 shard_map.191
  79.5 27.4 %all_to_all.66 = bf16[16,16,1536]{2,1,0:T(8,128)(2,1)S(1)} all-to-all(bf16[16,16,1536]{2,1,0:T(8,128)(2,1)S(1)} %bitcast.19), channel_id=1, replica_groups=mesh['chip'=8,'core'=2,'head'=16] {'head'}, dimensions={0} | all-to-all | bytes 1572864 | tf_op jit(solution)/shard_map/all_to_all | solution.py:480
  106.9 2.4 %shard_map.192 = (bf16[256,1536]{1,0:T(8,128)(2,1)S(1)}, bf16[16,96,688]{2,1,0:T(8,128)(2,1)S(1)}) custom-call(bf16[256,1536]{1,0:T(8,128)(2,1)S(1)} %bitcast.24, bf16[688,512]{1,0:T(8,128)(2,1)S(1)} %bitcast.27, bf16[688,512]{1,0:T(8,128)(2,1)S(1)} %bitcast.28, bf16[688,512]{1,0:T(8,128)(2,1)S(1)} %copy-done.43), custom_call_target="tpu_custom_call" | custom-call | flops 1623195648 | bytes 4194304 | tf_op jit(solution)/shard_map/pallas_call | solution.py:468
  109.4 1.4 copy-done.3
  110.8 26.9 %all_to_all.67 = bf16[16,16,1536]{2,1,0:T(8,128)(2,1)S(1)} all-to-all(bf16[16,16,1536]{2,1,0:T(8,128)(2,1)S(1)} %bitcast.25), channel_id=1, replica_groups=mesh['chip'=8,'core'=2,'head'=16] {'head'}, dimensions={0} | all-to-all | bytes 1572864 | tf_op jit(solution)/shard_map/all_to_all | solution.py:480
  138.7 6.5 %all-to-all-start.4 = ((bf16[16,16,1536]{2,1,0:T(8,128)(2,1)}), bf16[16,16,1536]{2,1,0:T(8,128)(2,1)S(1)}, u32[]{:S(2)}, u32[]{:S(2)}) async-start(bf16[16,16,1536]{2,1,0:T(8,128)(2,1)} %bitcast.10), calls=%async_computation.4 | async-start | bytes 1572864 | tf_op jit(solution)/shard_map/all_to_all | solution.py:480
  146.0 18.2 %all-to-all-done.4 = bf16[16,16,1536]{2,1,0:T(8,128)(2,1)S(1)} async-done(((bf16[16,16,1536]{2,1,0:T(8,128)(2,1)}), bf16[16,16,1536]{2,1,0:T(8,128)(2,1)S(1)}, u32[]{:S(2)}, u32[]{:S(2)}) %all-to-all-start.4) | async-done | bytes 786464 | tf_op jit(solution)/shard_map/all_to_all | solution.py:480
  165.2 1.5 shard_map.194.out_copies_ref
  166.7 4.7 %all-to-all-start.5 = ((bf16[8,272,256]{2,1,0:T(8,128)(2,1)}), bf16[8,272,256]{2,1,0:T(8,128)(2,1)S(1)}, u32[]{:S(2)}, u32[]{:S(2)}) async-start(bf16[8,272,256]{2,1,0:T(8,128)(2,1)} %shard_map.194.out_copies_ref), calls=%async_computation.5 | async-start | bytes 2228224 | tf_op jit(solution)/shard_map/all_to_all | solution.py:480
  180.5 4.8 %shard_map.195 = bf16[256,256]{1,0:T(8,128)(2,1)} custom-call(s32[32]{0:T(128)S(1)} %copy-done.39, s32[4]{0:T(128)S(1)} %copy-done.40, bf16[256,256]{1,0:T(8,128)(2,1)S(1)} %copy-done.25, bf16[256,256]{1,0:T(8,128)(2,1)S(1)} %copy-done.23, f32[2,256,128]{2,1,0:T(8,128)S(1)} %copy-done.30, bf16[8,272,256]{2,1,0:T(8,128)(2,1)} %shard_map.194.out_copies_ref, ...), custom_call_target="tpu_custom_call" | custom-call | flops 805306368 | bytes 6291456 | tf_op jit(solution)/shard_map/pallas_call | solution.py:468
  185.4 7.0 %all-to-all-done.5.mine_ref = bf16[8,272,256]{2,1,0:T(8,128)(2,1)S(1)} async-done(((bf16[8,272,256]{2,1,0:T(8,128)(2,1)}), bf16[8,272,256]{2,1,0:T(8,128)(2,1)S(1)}, u32[]{:S(2)}, u32[]{:S(2)}) %all-to-all-start.5) | async-done | bytes 1114144 | tf_op jit(solution)/shard_map/all_to_all | solution.py:480
  192.4 2.8 %collective-permute-done.9.other_ref = bf16[8,272,256]{2,1,0:T(8,128)(2,1)S(1)} collective-permute-done((bf16[8,272,256]{2,1,0:T(8,128)(2,1)S(1)}, bf16[8,272,256]{2,1,0:T(8,128)(2,1)S(1)}, u32[]{:S(2)}, u32[]{:S(2)}) %collective-permute-start.9) | collective-permute-done | bytes 1114144 | tf_op jit(solution)/shard_map/ppermute | solution.py:648
  196.2 4.9 %all-to-all-start.6 = ((bf16[16,96,256]{2,1,0:T(8,128)(2,1)}), bf16[16,96,256]{2,1,0:T(8,128)(2,1)S(1)}, u32[]{:S(2)}, u32[]{:S(2)}) async-start(bf16[16,96,256]{2,1,0:T(8,128)(2,1)} %copy-done.2), calls=%async_computation.6 | async-start | bytes 1572864 | tf_op jit(solution)/shard_map/all_to_all | solution.py:480
  201.2 1.6 copy-done.18
  202.8 1.3 copy-done.27
  204.0 4.6 %shard_map.197 = (bf16[256,256]{1,0:T(8,128)(2,1)}, bf16[256,256]{1,0:T(8,128)(2,1)}) custom-call(s32[32]{0:T(128)S(1)} %copy-done.39, s32[4]{0:T(128)S(1)} %copy-done.40, bf16[256,256]{1,0:T(8,128)(2,1)S(1)} %copy-done.35, bf16[256,256]{1,0:T(8,128)(2,1)S(1)} %copy-done.36, bf16[8,272,256]{2,1,0:T(8,128)(2,1)S(1)} %all-to-all-done.5.mine_ref, ...), custom_call_target="tpu_custom_call" | custom-call | flops 1073741824 | bytes 1073741824 | tf_op jit(solution)/shard_map/pallas_call | solution.py:468
  208.7 12.8 %reduce-scatter.2.cloned.1.call-done.held_ref = bf16[96,688]{1,0:T(8,128)(2,1)} async-done(((bf16[1536,688]{1,0:T(8,128)(2,1)}), bf16[96,688]{1,0:T(8,128)(2,1)}) %reduce-scatter.2.cloned.1.call-update) | async-done | bytes 132112 | tf_op jit(solution)/shard_map/reduce_scatter | solution.py:611
  (107 shorter events, 21.8 us)
Async XLA Ops:
  9.3 15.9 %collective-permute-start = (bf16[256,512]{1,0:T(8,128)(2,1)}, bf16[256,512]{1,0:T(8,128)(2,1)S(1)}, u32[]{:S(2)}, u32[]{:S(2)}) collective-permute-start(bf16[256,512]{1,0:T(8,128)(2,1)} %get-tuple-element.40.refs_0_), channel_id=1, source_target_pairs={{0,64},{16,80},{32,96},{48,112},{64,128},{80,144},{96,160},{112,17... | collective-permute-start | bytes 786440 | tf_op jit(solution)/shard_map/ppermute | solution.py:506
  10.9 14.3 %collective-permute-start.1 = (bf16[256,512]{1,0:T(8,128)(2,1)}, bf16[256,512]{1,0:T(8,128)(2,1)S(1)}, u32[]{:S(2)}, u32[]{:S(2)}) collective-permute-start(bf16[256,512]{1,0:T(8,128)(2,1)} %get-tuple-element.40.refs_0_), channel_id=1, source_target_pairs={{0,192},{16,208},{32,224},{48,240},{64,0},{80,16},{96,32},{112,48}... | collective-permute-start | bytes 786440 | tf_op jit(solution)/shard_map/ppermute | solution.py:506
  12.6 12.7 %collective-permute-start.2 = (bf16[256,512]{1,0:T(8,128)(2,1)}, bf16[256,512]{1,0:T(8,128)(2,1)S(1)}, u32[]{:S(2)}, u32[]{:S(2)}) collective-permute-start(bf16[256,512]{1,0:T(8,128)(2,1)} %get-tuple-element.40.refs_0_), channel_id=1, source_target_pairs={{0,32},{16,48},{32,0},{48,16},{64,96},{80,112},{96,64},{112,80},{1... | collective-permute-start | bytes 786440 | tf_op jit(solution)/shard_map/ppermute | solution.py:506
  13.8 21.6 %all-to-all-start = ((bf16[16,16,512]{2,1,0:T(8,128)(2,1)}), bf16[16,16,512]{2,1,0:T(8,128)(2,1)}, u32[]{:S(2)}, u32[]{:S(2)}) async-start(bf16[16,16,512]{2,1,0:T(8,128)(2,1)} %bitcast.29), calls=%async_computation | async-start | bytes 524288 | tf_op jit(solution)/shard_map/all_to_all | solution.py:480
  25.2 19.1 %copy-start.6 = (bf16[256,512]{1,0:T(8,128)(2,1)}, bf16[256,512]{1,0:T(8,128)(2,1)S(1)}, u32[]{:S(2)}) copy-start(bf16[256,512]{1,0:T(8,128)(2,1)S(1)} %collective-permute-done.1.refs_2_) | copy-start | bytes 786436
  25.3 19.1 %copy-start.8 = (bf16[256,512]{1,0:T(8,128)(2,1)}, bf16[256,512]{1,0:T(8,128)(2,1)S(1)}, u32[]{:S(2)}) copy-start(bf16[256,512]{1,0:T(8,128)(2,1)S(1)} %collective-permute-done.2.refs_3_) | copy-start | bytes 786436
  25.3 11.4 %collective-permute-start.3 = (bf16[256,512]{1,0:T(8,128)(2,1)S(1)}, bf16[256,512]{1,0:T(8,128)(2,1)S(1)}, u32[]{:S(2)}, u32[]{:S(2)}) collective-permute-start(bf16[256,512]{1,0:T(8,128)(2,1)S(1)} %collective-permute-done.refs_1_), channel_id=1, source_target_pairs={{0,32},{16,48},{32,0},{48,16},{64,96},{80,112},{96,64},{112,80},{1... | collective-permute-start | bytes 786440 | tf_op jit(solution)/shard_map/ppermute | solution.py:506
  26.2 10.4 %collective-permute-start.5 = (bf16[256,512]{1,0:T(8,128)(2,1)S(1)}, bf16[256,512]{1,0:T(8,128)(2,1)S(1)}, u32[]{:S(2)}, u32[]{:S(2)}) collective-permute-start(bf16[256,512]{1,0:T(8,128)(2,1)S(1)} %collective-permute-done.refs_1_), channel_id=1, source_target_pairs={{0,64},{16,80},{32,96},{48,112},{64,128},{80,144},{96,160},{112,17... | collective-permute-start | bytes 786440 | tf_op jit(solution)/shard_map/ppermute | solution.py:506
  26.5 14.9 %collective-permute-start.6 = (bf16[256,512]{1,0:T(8,128)(2,1)S(1)}, bf16[256,512]{1,0:T(8,128)(2,1)S(1)}, u32[]{:S(2)}, u32[]{:S(2)}) collective-permute-start(bf16[256,512]{1,0:T(8,128)(2,1)S(1)} %collective-permute-done.refs_1_), channel_id=1, source_target_pairs={{0,96},{16,112},{32,64},{48,80},{64,160},{80,176},{96,128},{112,14... | collective-permute-start | bytes 786440 | tf_op jit(solution)/shard_map/ppermute | solution.py:506
  28.8 12.7 %collective-permute-start.4 = (bf16[256,512]{1,0:T(8,128)(2,1)S(1)}, bf16[256,512]{1,0:T(8,128)(2,1)S(1)}, u32[]{:S(2)}, u32[]{:S(2)}) collective-permute-start(bf16[256,512]{1,0:T(8,128)(2,1)S(1)} %collective-permute-done.2.refs_3_), channel_id=1, source_target_pairs={{0,192},{16,208},{32,224},{48,240},{64,0},{80,16},{96,32},{112,48}... | collective-permute-start | bytes 786440 | tf_op jit(solution)/shard_map/ppermute | solution.py:506
  32.5 11.9 %copy-start.39 = (s32[32]{0:T(128)S(1)}, s32[32]{0:T(128)}, u32[]{:S(2)}) copy-start(s32[32]{0:T(128)} %order_ref.5) | copy-start | bytes 388
  32.5 11.9 %copy-start.40 = (s32[4]{0:T(128)S(1)}, s32[4]{0:T(128)}, u32[]{:S(2)}) copy-start(s32[4]{0:T(128)} %lens_ref.5) | copy-start | bytes 52
  32.5 9.2 %collective-permute-start.7 = (bf16[1024,512]{1,0:T(8,128)(2,1)}, bf16[1024,512]{1,0:T(8,128)(2,1)S(1)}, u32[]{:S(2)}, u32[]{:S(2)}) collective-permute-start(bf16[1024,512]{1,0:T(8,128)(2,1)} %shard_map.188), channel_id=1, source_target_pairs={{0,16},{16,0},{32,48},{48,32},{64,80},{80,64},{96,112},{112,96},{1... | collective-permute-start | bytes 3145736 | tf_op jit(solution)/shard_map/ppermute | solution.py:506
  36.6 13.2 %copy-start.10 = (bf16[256,512]{1,0:T(8,128)(2,1)}, bf16[256,512]{1,0:T(8,128)(2,1)S(1)}, u32[]{:S(2)}) copy-start(bf16[256,512]{1,0:T(8,128)(2,1)S(1)} %collective-permute-done.3.refs_0_.refs_4_) | copy-start | bytes 786436
  36.6 13.2 %copy-start.12 = (bf16[256,512]{1,0:T(8,128)(2,1)}, bf16[256,512]{1,0:T(8,128)(2,1)S(1)}, u32[]{:S(2)}) copy-start(bf16[256,512]{1,0:T(8,128)(2,1)S(1)} %collective-permute-done.5.refs_2_.refs_6_) | copy-start | bytes 786436
  41.6 2.7 %collective-permute-start.8 = (bf16[1024,512]{1,0:T(8,128)(2,1)S(1)}, bf16[1024,512]{1,0:T(8,128)(2,1)S(1)}, u32[]{:S(2)}, u32[]{:S(2)}) collective-permute-start(bf16[1024,512]{1,0:T(8,128)(2,1)S(1)} %shard_map.189), channel_id=1, source_target_pairs={{0,16},{16,0},{32,48},{48,32},{64,80},{80,64},{96,112},{112,96},{1... | collective-permute-start | bytes 3145736 | tf_op jit(solution)/shard_map/ppermute | solution.py:506
  50.5 113.6 %copy-start.21 = (bf16[256,256]{1,0:T(8,128)(2,1)}, bf16[256,256]{1,0:T(8,128)(2,1)S(1)}, u32[]{:S(2)}) copy-start(bf16[256,256]{1,0:T(8,128)(2,1)S(1)} %get-tuple-element.52.att_ref) | copy-start | bytes 393220
  51.3 27.0 %all-to-all-start.1 = ((bf16[16,16,1024]{2,1,0:T(8,128)(2,1)}), bf16[16,16,1024]{2,1,0:T(8,128)(2,1)S(1)}, u32[]{:S(2)}, u32[]{:S(2)}) async-start(bf16[16,16,1024]{2,1,0:T(8,128)(2,1)} %bitcast.26), calls=%async_computation.1 | async-start | bytes 1048576 | tf_op jit(solution)/shard_map/all_to_all | solution.py:480
  61.0 140.2 %all-gather.2.cloned.1.call-start = ((), (), s32[]{:S(2)}) async-start(), calls=%async_computation.8 | async-start | bytes 2228224 | tf_op jit(solution)/shard_map/all_gather | solution.py:570
  78.4 28.6 %copy-start.43 = (bf16[688,512]{1,0:T(8,128)(2,1)S(1)}, bf16[688,512]{1,0:T(8,128)(2,1)}, u32[]{:S(2)}) copy-start(bf16[688,512]{1,0:T(8,128)(2,1)} %dl_ref.1) | copy-start | bytes 2113540
  79.5 27.4 %copy-start.41 = (bf16[512,688]{0,1:T(8,128)(2,1)S(1)}, bf16[512,688]{0,1:T(8,128)(2,1)}, u32[]{:S(2)}) copy-start(bf16[512,688]{0,1:T(8,128)(2,1)} %param.18) | copy-start | bytes 2113540
  79.5 27.4 %copy-start.42 = (bf16[512,688]{0,1:T(8,128)(2,1)S(1)}, bf16[512,688]{0,1:T(8,128)(2,1)}, u32[]{:S(2)}) copy-start(bf16[512,688]{0,1:T(8,128)(2,1)} %param.19) | copy-start | bytes 2113540
  138.7 25.5 %all-to-all-start.4 = ((bf16[16,16,1536]{2,1,0:T(8,128)(2,1)}), bf16[16,16,1536]{2,1,0:T(8,128)(2,1)S(1)}, u32[]{:S(2)}, u32[]{:S(2)}) async-start(bf16[16,16,1536]{2,1,0:T(8,128)(2,1)} %bitcast.10), calls=%async_computation.4 | async-start | bytes 1572864 | tf_op jit(solution)/shard_map/all_to_all | solution.py:480
  145.3 76.2 %reduce-scatter.2.cloned.1.call-start = ((), (), s32[]{:S(2)}) async-start(), calls=%async_computation.9 | async-start | bytes 2506752 | tf_op jit(solution)/shard_map/reduce_scatter | solution.py:611
  145.3 18.9 %copy-start.19 = (bf16[256,256]{1,0:T(8,128)(2,1)S(1)}, bf16[256,256]{1,0:T(8,128)(2,1)}, u32[]{:S(2)}) copy-start(bf16[256,256]{1,0:T(8,128)(2,1)} %og_ref.5) | copy-start | bytes 393220
  145.3 18.9 %copy-start.29 = (f32[2,256,128]{2,1,0:T(8,128)S(1)}, f32[2,256,128]{2,1,0:T(8,128)}, u32[]{:S(2)}) copy-start(f32[2,256,128]{2,1,0:T(8,128)} %copy-done.28) | copy-start | bytes 786436
  145.3 18.9 %copy-start.32 = (bf16[256,512]{1,0:T(8,128)(2,1)S(1)}, bf16[256,512]{1,0:T(8,128)(2,1)}, u32[]{:S(2)}) copy-start(bf16[256,512]{1,0:T(8,128)(2,1)} %gl_ref.3) | copy-start | bytes 786436
  166.7 25.7 %all-to-all-start.5 = ((bf16[8,272,256]{2,1,0:T(8,128)(2,1)}), bf16[8,272,256]{2,1,0:T(8,128)(2,1)S(1)}, u32[]{:S(2)}, u32[]{:S(2)}) async-start(bf16[8,272,256]{2,1,0:T(8,128)(2,1)} %shard_map.194.out_copies_ref), calls=%async_computation.5 | async-start | bytes 2228224 | tf_op jit(solution)/shard_map/all_to_all | solution.py:480
  185.4 15.8 %copy-start.35 = (bf16[256,256]{1,0:T(8,128)(2,1)S(1)}, bf16[256,256]{1,0:T(8,128)(2,1)}, u32[]{:S(2)}) copy-start(bf16[256,256]{1,0:T(8,128)(2,1)} %k_ref.3) | copy-start | bytes 393220
  185.4 15.8 %copy-start.36 = (bf16[256,256]{1,0:T(8,128)(2,1)S(1)}, bf16[256,256]{1,0:T(8,128)(2,1)}, u32[]{:S(2)}) copy-start(bf16[256,256]{1,0:T(8,128)(2,1)} %v_ref.3) | copy-start | bytes 393220
  192.4 2.8 %collective-permute-start.9 = (bf16[8,272,256]{2,1,0:T(8,128)(2,1)S(1)}, bf16[8,272,256]{2,1,0:T(8,128)(2,1)S(1)}, u32[]{:S(2)}, u32[]{:S(2)}) collective-permute-start(bf16[8,272,256]{2,1,0:T(8,128)(2,1)S(1)} %all-to-all-done.5.mine_ref), channel_id=1, source_target_pairs={{0,16},{16,0},{1,17},{17,1},{2,18},{18,2},{3,19},{19,3},{4,20},{20... | collective-permute-start | bytes 3342344 | tf_op jit(solution)/shard_map/ppermute | solution.py:648
  196.2 26.9 %all-to-all-start.6 = ((bf16[16,96,256]{2,1,0:T(8,128)(2,1)}), bf16[16,96,256]{2,1,0:T(8,128)(2,1)S(1)}, u32[]{:S(2)}, u32[]{:S(2)}) async-start(bf16[16,96,256]{2,1,0:T(8,128)(2,1)} %copy-done.2), calls=%async_computation.6 | async-start | bytes 1572864 | tf_op jit(solution)/shard_map/all_to_all | solution.py:480
  (29 other events, 69.7 us)
Sparse Core Ops, SparseCore 0:
  63.7 37.9 all-gather.1
  148.6 72.7 reduce-scatter.1
